TPU v7x, 256 devices: a whole 4x4x8 slice. The times are simulated.
256 devices in a mesh: context: 64 (over y, z, core), tensor: 4 (over x).
Axes of the slice: x: 4, y: 4, z: 8, core: 2. Of those that a mesh axis runs over, the one named last changes fastest.
Arguments:
- layer_input: bfloat16 [32768, 1024], P('context', 'tensor'), may hold values from -16 to 16
- value_proj: bfloat16 [1024, 2048], P(None, 'tensor'), may hold values from -0.1875 to 0.1875
- conv_taps: float32 [4, 2048], P(None, 'tensor'), may hold values from -3 to 3
- conv_pre: bfloat16 [32768, 2048], P('context', 'tensor'), may hold values from -6 to 6
- state_in: bfloat16 [32768, 128], P('context'), may hold values from -6 to 6
- state_out: bfloat16 [32768, 128], P('context'), may hold values from -0.5 to 0.5
- step_size: float32 [32, 32768], P('tensor', 'context'), may hold values from 0 to 1
- log_decay: float32 [32, 32768], P('tensor', 'context'), may hold values from -2 to 0
- skip_gain: float32 [32], P('tensor'), may hold values from 0.5 to 2
- grad_out: bfloat16 [32768, 2048], P('context', 'tensor'), may hold values from -6 to 6
Outputs:
- grad_input: bfloat16 [32768, 1024], P('context', 'tensor')
- grad_value_proj: float32 [1024, 2048], P('context', 'tensor')
All inputs are finite; a program needn't handle non-finite values.
Results may differ from a plain program's by a relative error of at most 0.0059.
Values may be sent and summed in bfloat16 or wider, within the bound.
A program may use at most 64 MiB of HBM per device.

v0:
```python
import math

import jax
import jax.numpy as jnp
from jax import lax
from jax.sharding import PartitionSpec as P

CONV = 4
BLOCK = 256


def prefix(part, axis, combine, identity):
    count = lax.axis_size(axis)
    place = lax.axis_index(axis)
    ahead = count - 1 - place
    gathered = jax.tree.map(lambda a: lax.all_gather(a, axis), part)
    state = jax.tree.map(lambda a, e: jnp.zeros_like(a) + jnp.asarray(e, a.dtype), part, identity)

    def one(hop, state):
        source = count - 1 - hop
        return combine(
            state, jax.tree.map(lambda a: lax.dynamic_index_in_dim(a, source, 0, False), gathered)
        )

    return lax.fori_loop(0, ahead, one, state)


def from_behind(value, axis, steps):
    count = lax.axis_size(axis)
    leading, last = (max(0, -steps), min(count, count - steps))
    return lax.ppermute(value, axis, [(source, source + steps) for source in range(leading, last)])


def silu_slope(values):
    sigmoid_value = jax.nn.sigmoid(values)
    return sigmoid_value * (1.0 + values * (1.0 - sigmoid_value))


def within_part(input_blk, output_blk, grad_blk, cumulative_blk):
    length = input_blk.shape[0]
    scores = lax.dot_general(
        input_blk, output_blk, (((1,), (1,)), ((), ())), preferred_element_type=jnp.float32
    )
    spread = cumulative_blk[:, None, :] - cumulative_blk[:, :, None]
    upper_mask = jnp.arange(length)[None, :] >= jnp.arange(length)[:, None]
    damping = jnp.where(upper_mask[None], jnp.exp(jnp.minimum(spread, 0.0)), 0.0)
    weights = (scores[None] * damping).astype(jnp.bfloat16)
    return jnp.einsum("hts,shp->thp", weights, grad_blk, preferred_element_type=jnp.float32)


def beyond_part(carried, input_blk, cumulative_blk):
    closing = cumulative_blk[:, -1:]
    beyond = jnp.einsum(
        "hpn,tn->thp", carried.astype(jnp.bfloat16), input_blk, preferred_element_type=jnp.float32
    )
    return beyond * jnp.exp(closing - cumulative_blk).T[:, :, None]


def carry_in(total_decay, local_state):

    def combine(earlier_part, later_part):
        return (
            later_part[0] + earlier_part[0],
            later_part[1] + jnp.exp(later_part[0])[:, None, None] * earlier_part[1],
        )

    identity = (jnp.zeros_like(total_decay), jnp.zeros_like(local_state))
    result = prefix((total_decay, local_state), "context", combine, identity)
    return result[1]


def local(
    layer_input,
    value_proj,
    conv_taps,
    conv_pre,
    state_in,
    state_out,
    step_size,
    log_decay,
    skip_gain,
    grad_out,
):
    gathered = lax.all_gather(layer_input, "tensor", axis=1, tiled=True)
    row_count, inner_width = grad_out.shape
    head_count = step_size.shape[0]
    head_width = inner_width // head_count
    state_width = state_in.shape[1]
    block_count = row_count // BLOCK
    input_blocks = state_in.reshape(block_count, BLOCK, state_width)
    output_blocks = state_out.reshape(block_count, BLOCK, state_width)
    grad_blocks = grad_out.reshape(block_count, BLOCK, head_count, head_width)
    step_blocks = step_size.reshape(head_count, block_count, BLOCK).transpose(1, 0, 2)
    running_total = jnp.cumsum(log_decay.reshape(head_count, block_count, BLOCK), axis=2).transpose(
        1, 0, 2
    )
    closings = running_total[:, :, -1]
    weighted = (
        grad_blocks.astype(jnp.float32) * jnp.exp(running_total).transpose(0, 2, 1)[:, :, :, None]
    ).astype(jnp.bfloat16)
    block_states = jnp.einsum(
        "kshp,ksn->khpn", weighted, output_blocks, preferred_element_type=jnp.float32
    )
    before = jnp.cumsum(closings, axis=0) - closings
    local_state = jnp.sum(jnp.exp(before)[:, :, None, None] * block_states, axis=0)
    incoming = carry_in(jnp.sum(closings, axis=0), local_state)

    def whole_increment(carried, pieces):
        input_blk, output_blk, grad_blk, step_blk, cumulative_blk, state_blk = pieces
        within = within_part(input_blk, output_blk, grad_blk, cumulative_blk)
        beyond = beyond_part(carried, input_blk, cumulative_blk)
        grad_block = step_blk.T[:, :, None] * (within + beyond) + skip_gain[
            None, :, None
        ] * grad_blk.astype(jnp.float32)
        carried = jnp.exp(cumulative_blk[:, -1])[:, None, None] * carried + state_blk
        return (carried, grad_block)

    block_inputs = (
        input_blocks,
        output_blocks,
        grad_blocks,
        step_blocks,
        running_total,
        block_states,
    )
    grad_x = lax.scan(whole_increment, incoming, block_inputs, reverse=True)[1].reshape(
        row_count, inner_width
    )
    grad_conv = (grad_x * silu_slope(conv_pre.astype(jnp.float32))).astype(jnp.bfloat16)
    subsequent = from_behind(grad_conv[: CONV - 1], "context", -1)
    extended = jnp.concatenate([grad_conv, subsequent], axis=0).astype(jnp.float32)
    summed = jnp.zeros((row_count, inner_width), jnp.float32)
    for offset in range(CONV):
        start_row = CONV - 1 - offset
        summed = summed + conv_taps[offset][None, :] * extended[start_row : start_row + row_count]
    grad_proj = summed.astype(jnp.bfloat16)
    context_count = lax.axis_size("context")
    scaling = 1.0 / math.sqrt(row_count * context_count)
    product = lax.dot_general(
        gathered, grad_proj, (((0,), (0,)), ((), ())), preferred_element_type=jnp.float32
    )
    grad_value_proj = lax.psum_scatter(
        product * scaling, "context", scatter_dimension=0, tiled=True
    )
    partial_input = lax.dot_general(
        grad_proj, value_proj, (((1,), (1,)), ((), ())), preferred_element_type=jnp.float32
    )
    grad_input = lax.psum_scatter(partial_input, "tensor", scatter_dimension=1, tiled=True).astype(
        jnp.bfloat16
    )
    return (grad_input, grad_value_proj)


def solution(mesh):
    return jax.shard_map(
        local,
        mesh=mesh,
        in_specs=(
            P("context", "tensor"),
            P(None, "tensor"),
            P(None, "tensor"),
            P("context", "tensor"),
            P("context", None),
            P("context", None),
            P("tensor", "context"),
            P("tensor", "context"),
            P("tensor"),
            P("context", "tensor"),
        ),
        out_specs=(P("context", "tensor"), P("context", "tensor")),
        check_vma=False,
    )
```

profile of v0, /device:TPU:1, one launch (start us, length us, event | category | flops | bytes accessed | tf_op | source)
XLA Modules:
  0.0 429.8 jit_solution(11256449267206146731)
XLA Ops:
  8.0 1.1 reduce-window.6
  9.8 1.3 copy.57
  11.6 1.9 multiply_reduce_fusion
  16.9 129.4 %all-reduce = f32[512]{0:T(512)S(1)} all-reduce(f32[512]{0:T(512)S(1)} %dynamic-update-slice), channel_id=3, replica_groups=mesh['context'=64,'tensor'=4] {'context'}, use_global_device_ids=true, to_apply=%add | all-reduce | flops 512 | bytes 4096
  147.4 68.8 %while.30 = (s32[]{:T(128)}, f32[8,64,128]{2,1,0:T(8,128)S(1)}, s32[]{:T(128)}, f32[64,8,64,128]{3,2,1,0:T(8,128)}, f32[64,8]{1,0:T(8,128)S(1)}, /*index=5*/s32[]{:T(128)}, s32[]{:T(128)}, s32[]{:T(128)}, s32[]{:T(128)}) while((s32[]{:T(128)}, f32[8,64,128]{2,1,0:T(8,128)S(1)}, s32[]{:T(128)}, f32[64,8,64,128]{3,2,1,0:T(8,128)}, ...), condition=%wide.region_6.7_spmd, body=%wide.region_5.6_spmd.sunk | while | flops 131078 | bytes 786675 | solution.py:25
  147.4 1.1 bitcast_add_fusion.4
  148.5 1.1 bitcast_add_fusion.4
  149.6 1.1 bitcast_add_fusion.4
  150.7 1.1 bitcast_add_fusion.4
  151.9 1.1 bitcast_add_fusion.4
  153.0 1.1 bitcast_add_fusion.4
  154.1 1.1 bitcast_add_fusion.4
  155.2 1.1 bitcast_add_fusion.4
  156.3 1.1 bitcast_add_fusion.4
  157.4 1.1 bitcast_add_fusion.4
  158.5 1.1 bitcast_add_fusion.4
  159.6 1.1 bitcast_add_fusion.4
  160.7 1.1 bitcast_add_fusion.4
  161.8 1.1 bitcast_add_fusion.4
  165.2 1.1 bitcast_add_fusion.4
  170.7 1.1 bitcast_add_fusion.4
  174.0 1.1 bitcast_add_fusion.4
  177.4 1.1 bitcast_add_fusion.4
  179.6 1.1 bitcast_add_fusion.4
  182.9 1.1 bitcast_add_fusion.4
  186.2 1.1 bitcast_add_fusion.4
  191.8 1.1 bitcast_add_fusion.4
  195.1 1.1 bitcast_add_fusion.4
  198.4 1.1 bitcast_add_fusion.4
  200.6 1.1 bitcast_add_fusion.4
  204.0 1.1 bitcast_add_fusion.4
  207.3 1.1 bitcast_add_fusion.4
  212.8 1.1 bitcast_add_fusion.4
  216.4 25.9 %while.31 = (s32[]{:T(128)}, f32[8,64,128]{2,1,0:T(8,128)S(1)}, f32[2,256,8,64]{1,0,3,2:T(2,128)S(1)}, f32[2,8,256]{2,1,0:T(8,128)S(1)}, f32[2,8,64,128]{3,2,1,0...) while((s32[]{:T(128)}, f32[8,64,128]{2,1,0:T(8,128)S(1)}, ...), condition=%wide.region_8.9_spmd, body=%wide.region_7.8_spmd.sunk | while | flops 121112576 | bytes 6228345 | solution.py:126
  216.7 1.1 convolution_multiply_fusion.2
  219.6 1.8 fusion.63
  221.9 7.3 %dynamic_update_slice.11 = f32[2,256,8,64]{1,0,3,2:T(2,128)S(1)} dynamic-update-slice(f32[2,256,8,64]{1,0,3,2:T(2,128)S(1)} %get-tuple-element.496, f32[1,256,8,64]{1,0,3,2:T(1,128)S(1)} %copy.90, s32[]{:T(128)S(6)} %sub.113, s32[]{:T(128)} %constant.103.clone.1..sunk.1, s32[]{:T(128)} %constant.103.clone.1..sunk.1, s32[]{:T(128)} %constant.103.clone.1..sunk.1) | dynamic-update-slice | bytes 1048580 | tf_op jit(solution)/shard_map/while/body/jit(dynamic_update_index_in_dim)/dynamic_update_slice | solution.py:126
  229.6 1.1 convolution_multiply_fusion.2
  232.5 1.8 fusion.63
  234.9 7.3 %dynamic_update_slice.11 = f32[2,256,8,64]{1,0,3,2:T(2,128)S(1)} dynamic-update-slice(f32[2,256,8,64]{1,0,3,2:T(2,128)S(1)} %get-tuple-element.496, f32[1,256,8,64]{1,0,3,2:T(1,128)S(1)} %copy.90, s32[]{:T(128)S(6)} %sub.113, s32[]{:T(128)} %constant.103.clone.1..sunk.1, s32[]{:T(128)} %constant.103.clone.1..sunk.1, s32[]{:T(128)} %constant.103.clone.1..sunk.1) | dynamic-update-slice | bytes 1048580 | tf_op jit(solution)/shard_map/while/body/jit(dynamic_update_index_in_dim)/dynamic_update_slice | solution.py:126
  243.8 8.0 %collective-permute-start = (bf16[3,512]{0,1:T(8,128)(2,1)S(1)}, bf16[3,512]{0,1:T(8,128)(2,1)S(1)}, u32[]{:S(2)}, u32[]{:S(2)}) collective-permute-start(bf16[3,512]{0,1:T(8,128)(2,1)S(1)} %slice.62), channel_id=1, source_target_pairs={{4,0},{8,4},{12,8},{16,12},{20,16},{24,20},{28,24},{32,28},{36,32}... | collective-permute-start | bytes 9224 | tf_op jit(solution)/shard_map/ppermute | solution.py:31
  252.9 1.3 fusion.32
  255.0 2.1 fusion.39
  257.2 2.1 multiply_bitcast_fusion
  259.3 1.8 copy.66
  261.2 21.7 %reduce-scatter.5.cloned.1.call-done = f32[512,256]{1,0:T(8,128)} async-done(((f32[512,1024]{1,0:T(8,128)}), f32[512,256]{1,0:T(8,128)}) %reduce-scatter.5.cloned.1.call-update) | async-done | bytes 524304 | tf_op jit(solution)/shard_map/reduce_scatter | solution.py:148
  282.9 1.8 convert_element_type.54
  284.6 138.6 %reduce-scatter.7.cloned.1.call-done = f32[16,512]{1,0:T(8,128)} async-done(((f32[1024,512]{1,0:T(8,128)}), f32[16,512]{1,0:T(8,128)}) %reduce-scatter.7.cloned.1.call-update) | async-done | bytes 32784
  (170 shorter events, 51.6 us)
Async XLA Ops:
  7.2 247.8 %copy-start = (bf16[1024,512]{1,0:T(8,128)(2,1)S(1)}, bf16[1024,512]{1,0:T(8,128)(2,1)}, u32[]{:S(2)}) copy-start(bf16[1024,512]{1,0:T(8,128)(2,1)} %param.15) | copy-start | bytes 3145732
  7.2 140.2 %all-gather.7.cloned.1.call-start = ((), (), s32[]{:S(2)}) async-start(), calls=%async_computation.4 | async-start | bytes 17039360 | tf_op jit(solution)/shard_map/all_gather | solution.py:16
  11.2 4.1 copy-start.5
  11.2 135.1 %copy-start.3 = (bf16[512,512]{1,0:T(8,128)(2,1)S(1)}, bf16[512,512]{1,0:T(8,128)(2,1)}, u32[]{:S(2)}) copy-start(bf16[512,512]{1,0:T(8,128)(2,1)} %param.17) | copy-start | bytes 1572868
  13.6 243.6 %all-gather.5.cloned.1.call-start = ((), (), s32[]{:S(2)}) async-start(), calls=%async_computation.3 | async-start | bytes 1310720 | tf_op jit(solution)/shard_map/all_gather | solution.py:84
  14.3 268.5 %reduce-scatter.5.cloned.1.call-start = ((), (), s32[]{:S(2)}) async-start(), calls=%async_computation.2 | async-start | bytes 2621440 | tf_op jit(solution)/shard_map/reduce_scatter | solution.py:148
  242.3 1.0 copy-start.2
  242.3 9.5 %copy-start.4 = (f32[4,512]{1,0:T(4,128)S(1)}, f32[4,512]{1,0:T(4,128)}, u32[]{:S(2)}) copy-start(f32[4,512]{1,0:T(4,128)} %param.16) | copy-start | bytes 24580
  243.8 9.0 %collective-permute-start = (bf16[3,512]{0,1:T(8,128)(2,1)S(1)}, bf16[3,512]{0,1:T(8,128)(2,1)S(1)}, u32[]{:S(2)}, u32[]{:S(2)}) collective-permute-start(bf16[3,512]{0,1:T(8,128)(2,1)S(1)} %slice.62), channel_id=1, source_target_pairs={{4,0},{8,4},{12,8},{16,12},{20,16},{24,20},{28,24},{32,28},{36,32}... | collective-permute-start | bytes 9224 | tf_op jit(solution)/shard_map/ppermute | solution.py:31
  254.2 0.8 copy-start.1
  257.1 166.1 %reduce-scatter.7.cloned.1.call-start = ((), (), s32[]{:S(2)}) async-start(), calls=%async_computation.5 | async-start | bytes 2129920
Sparse Core Ops, SparseCore 0:
  13.7 104.3 all-gather.6
  119.9 24.1 all-gather.4
  257.2 25.5 reduce-scatter.4
  287.9 135.3 reduce-scatter.6
where the time goes:
time: 437 us; the launch traced here: 430 us
  waiting for transfers between devices  162 us (37%)
  blocking collectives  129 us (30%)
  other arithmetic  71.6 us (16%)
  local copies, waits for them, and re-layouts  27.5 us (6%)
  between operations  14.6 us (3%)
  matrix products  14 us (3%)
  starting transfers between devices  8.21 us (2%)
    unnamed x5, waiting for transfers between devices  139 us
    unnamed x1, blocking collectives  129 us
    add x62, other arithmetic, combine(): later_part[1] + jnp.exp(later_part[0])[:, None, None] * earlier_part[1]  65.8 us
    reduce_scatter x1, waiting for transfers between devices, local(): lax.psum_scatter(partial_input, 'tensor', scatter_dimension=1, tiled=True)  21.7 us
    dynamic_update_slice x4, local copies, waits for them, and re-layouts, local(): lax.scan(whole_increment, incoming, block_inputs, reverse=True)[1]  15.6 us
  transfers between devices with their start and end apart: 5, of which 3 were waited for; matrix products, arithmetic and copies ran while one was open for 24% of the time, Pallas kernels for 0%

commit v1 on v0

v1 whole, which is shorter than its diff:
```python
import functools
import math

import jax
import jax.numpy as jnp
from jax import lax
from jax.experimental import pallas as pl
from jax.experimental.pallas import tpu as pltpu
from jax.sharding import PartitionSpec as P

MESH = pl.DeviceIdType.MESH
F32, BF16 = jnp.float32, jnp.bfloat16
HIGH = lax.Precision.HIGHEST

NX, NY, NZ, NC = 4, 4, 8, 2
NROW = NZ * NC
NCTX = NY * NROW
ROWS, CH, STATE, BLOCK, HEADS, HD = 512, 512, 128, 256, 8, 64
FEAT = 256
Q, QW = 2, 256
TILE, NT = 128, 4


def dot(a, b, dims, precision=None):
    return lax.dot_general(a, b, (dims, ((), ())), precision=precision, preferred_element_type=F32)


def remote(src, dst, send, recv, ctx, ten):
    return pltpu.make_async_remote_copy(
        src_ref=src, dst_ref=dst, send_sem=send, recv_sem=recv,
        device_id=(ctx, ten), device_id_type=MESH,
    )


def kernel(
    lay_h, vp_h, taps_h, pre_h, sin_h, sout_h, step_h, ld_h, skip_h, go_h,
    gi_ref, gv_ref,
    lay, vp, taps, pre, sin, sout, step, ld, skip, go,
    cum, a_ref, b_ref, gc, gp, bs1, clos, lt,
    s_send, s_recv, d_send, d_recv, rsuf, lsuf, y_send, y_recv, c_send, carry,
    p_send, x_recv, x_own,
    w_send, w_recv, w_own, v_send, v_recv, u_own, u_send, u_recv,
    in_sem, lay_ss, lay_rs, s_ss, s_rs, d_ss, d_rs, y_ss, y_rs, c_ss, c_rs, h_ss, h_rs,
    x_ss, x_rs, w_ss, w_rs, v_ss, v_rs, u_ss, u_rs,
):
    c = lax.axis_index("context")
    t = lax.axis_index("tensor")
    core = lax.rem(c, NC)
    z = lax.rem(c // NC, NZ)
    y = c // NROW
    i = lax.rem(c, NROW)
    row0 = y * NROW
    nxt, prv = lax.rem(c + 1, NCTX), lax.rem(c + NCTX - 1, NCTX)

    barrier = pltpu.get_barrier_semaphore()

    def greet(ctx, ten):
        pl.semaphore_signal(barrier, inc=1, device_id=(ctx, ten), device_id_type=MESH)

    def greet_row(k, _):
        greet(row0 + lax.rem(i + k, NROW), t)
        return 0

    lax.fori_loop(1, NROW, greet_row, 0)
    for k in range(1, NY):
        greet(lax.rem(c + k * NROW, NCTX), t)
    for k in range(1, NX):
        greet(c, lax.rem(t + k, NX))
    greet(nxt, t)
    greet(prv, t)

    loads = {}
    for n, (name, src, dst) in enumerate((
        ("ld", ld_h, ld), ("go", go_h, go), ("sout", sout_h, sout), ("sin", sin_h, sin),
        ("step", step_h, step), ("skip", skip_h, skip), ("pre", pre_h, pre), ("taps", taps_h, taps),
        ("vp", vp_h, vp), ("lay", lay_h, lay.at[t]),
    )):
        loads[name] = pltpu.make_async_copy(src, dst, in_sem.at[n])
        loads[name].start()

    ri = lax.broadcasted_iota(jnp.int32, (BLOCK, BLOCK), 0)
    ci = lax.broadcasted_iota(jnp.int32, (BLOCK, BLOCK), 1)
    upto = (ri <= ci).astype(F32)
    hi = lax.broadcasted_iota(jnp.int32, (HEADS, CH), 0)
    li = lax.broadcasted_iota(jnp.int32, (HEADS, CH), 1)
    onehot = (li // HD == hi).astype(F32)
    loads["ld"].wait()
    for k in range(2):
        cum[:, k * BLOCK:(k + 1) * BLOCK] = dot(ld[:, k * BLOCK:(k + 1) * BLOCK], upto, ((1,), (0,)), HIGH)
    for k in range(2):
        b_ref[k * BLOCK:(k + 1) * BLOCK, :] = dot(cum[:, k * BLOCK:(k + 1) * BLOCK], onehot, ((0,), (0,)), HIGH)
    clos0 = b_ref[BLOCK - 1:BLOCK, :]
    clos1 = b_ref[2 * BLOCK - 1:2 * BLOCK, :]
    clos[0:1, :] = clos0
    clos[1:2, :] = clos1
    for k in range(NC):
        d_send[k] = (clos0 + clos1)[:, k * 256:(k + 1) * 256]

    pl.semaphore_wait(barrier, NROW - 1 + NY - 1 + NX - 1 + 2)

    def d_copy(k):
        j = lax.rem(i + k, NROW)
        return remote(d_send.at[lax.rem(j, NC)], d_recv.at[i], d_ss.at[j], d_rs.at[i], row0 + j, t)

    def start_d(k, _):
        d_copy(k).start()
        return 0

    lax.fori_loop(1, NROW, start_d, 0)
    d_recv[i] = d_send[core]

    for k in (1, 3, 2):
        tt = lax.rem(t + k, NX)
        remote(lay_h, lay.at[t], lay_ss.at[tt], lay_rs.at[t], c, tt).start()

    loads["go"].wait()
    loads["sout"].wait()
    state = None
    for k in range(2):
        w = (go[k * BLOCK:(k + 1) * BLOCK, :].astype(F32) * jnp.exp(b_ref[k * BLOCK:(k + 1) * BLOCK, :])).astype(BF16)
        bs = dot(sout[k * BLOCK:(k + 1) * BLOCK, :], w, ((0,), (0,)))
        if k == 0:
            state = bs
        else:
            bs1[...] = bs
            state = state + jnp.exp(clos0) * bs
    state = state.astype(BF16)
    for k in range(NC):
        s_send[k] = state[:, k * 256:(k + 1) * 256]

    def s_copy(k):
        j = lax.rem(i + k, NROW)
        rows = pl.ds(pl.multiple_of((j // NC) * 16, 16), 16)
        return remote(s_send.at[lax.rem(j, NC), rows], s_recv.at[i], s_ss.at[j], s_rs.at[i], row0 + j, t)

    def start_s(k, _):
        s_copy(k).start()
        return 0

    lax.fori_loop(1, NROW, start_s, 0)
    s_recv[i] = s_send[core, pl.ds(pl.multiple_of(z * 16, 16), 16), :]

    for name in ("sin", "step", "skip", "pre"):
        loads[name].wait()
    skip_e = dot(skip[...], onehot, ((1,), (0,)), HIGH)

    def within(k):
        r0 = k * BLOCK
        rows = slice(r0, r0 + BLOCK)
        scores = dot(sin[rows, :], sout[rows, :], ((1,), (1,)))
        scores = jnp.where(ci >= ri, scores, 0.0)
        low = lax.broadcasted_iota(jnp.int32, (BLOCK, 128), 1) < HD
        cum_t = cum[:, rows].T
        for pair in range(HEADS // 2):
            lanes = slice(pair * 128, pair * 128 + 128)
            g = go[rows, lanes]
            parts = []
            for h in (2 * pair, 2 * pair + 1):
                spread = cum[h:h + 1, rows] - cum_t[:, h:h + 1]
                weights = (scores * jnp.exp(jnp.minimum(spread, 0.0))).astype(BF16)
                parts.append(dot(weights, g, ((1,), (0,))))
            a_ref[rows, lanes] = jnp.where(low, parts[0], parts[1])

    within(0)

    def d_wait(k, _):
        j = lax.rem(i + k, NROW)
        remote(d_send.at[0], d_recv.at[j], d_ss.at[j], d_rs.at[j], c, t).wait_recv()
        return 0

    def s_wait(k, _):
        j = lax.rem(i + k, NROW)
        remote(s_send.at[0, pl.ds(0, 16)], s_recv.at[j], s_ss.at[j], s_rs.at[j], c, t).wait_recv()
        return 0

    lax.fori_loop(1, NROW, d_wait, 0)
    lax.fori_loop(1, NROW, s_wait, 0)

    def scan(k, carried):
        r, l = carried
        j = NROW - 1 - k
        rsuf[j] = r
        lsuf[j] = l
        d = d_recv[j]
        return (s_recv[j].astype(F32) + jnp.exp(d) * r, l + d)

    total, span = lax.fori_loop(0, NROW, scan, (jnp.zeros((16, 256), F32), jnp.zeros((1, 256), F32)))
    y_send[0:16, :] = total
    y_send[16:24, :] = jnp.broadcast_to(span, (8, 256))
    for k in range(1, NY):
        yy = lax.rem(y + k, NY)
        remote(y_send, y_recv.at[y], y_ss.at[yy], y_rs.at[y], lax.rem(c + k * NROW, NCTX), t).start()
    y_recv[y] = y_send[...]

    within(1)

    for k in range(1, NY):
        yy = lax.rem(y + k, NY)
        remote(y_send, y_recv.at[yy], y_ss.at[yy], y_rs.at[yy], c, t).wait_recv()
    coming = jnp.zeros((16, 256), F32)
    for yy in range(NY - 1, 0, -1):
        r = y_recv[yy]
        coming = jnp.where(yy > y, r[0:16, :] + jnp.exp(r[16:17, :]) * coming, coming)

    my_rows = pl.ds(pl.multiple_of(z * 16, 16), 16)

    def c_copy(k):
        j = lax.rem(i + k, NROW)
        return remote(c_send.at[j], carry.at[core, my_rows], c_ss.at[j], c_rs.at[i], row0 + j, t)

    def start_c(k, _):
        j = lax.rem(i + k, NROW)
        c_send[j] = (rsuf[j] + jnp.exp(lsuf[j]) * coming).astype(BF16)
        c_copy(k).start()
        return 0

    lax.fori_loop(1, NROW, start_c, 0)
    carry[core, my_rows, :] = (rsuf[i] + jnp.exp(lsuf[i]) * coming).astype(BF16)

    for k in range(2):
        close = clos[k:k + 1, :]

        def factors(n, _, k=k, close=close):
            rows = pl.ds(pl.multiple_of(k * BLOCK + n * 64, 64), 64)
            v = pre[rows, :].astype(F32)
            sig = 1.0 / (1.0 + jnp.exp(-v))
            slope = sig * (1.0 + v * (1.0 - sig))
            step_e = dot(step_t(k * BLOCK + n * 64), onehot, ((0,), (0,)), HIGH)
            a_ref[rows, :] = (step_e * a_ref[rows, :] + skip_e * go[rows, :].astype(F32)) * slope
            b_ref[rows, :] = step_e * jnp.exp(close - b_ref[rows, :]) * slope
            return 0

        def step_t(start):
            return step[:, start:start + 64]

        for n in range(4):
            factors(n, 0)

    loads["lay"].wait()
    for k in range(1, NX):
        tt = lax.rem(t + k, NX)
        remote(lay_h, lay.at[tt], lay_ss.at[tt], lay_rs.at[tt], c, tt).wait_recv()

    def transposed(x, _):
        for half in range(2):
            cols = slice(half * 256, half * 256 + 256)
            tr = lay[x, cols, :].T
            for zz in range(NZ):
                for cc in range(NC):
                    f0 = (zz * NC + cc) * 16
                    lt[cc, pl.ds(pl.multiple_of(x * 128 + zz * 16, 16), 16), cols] = tr[f0:f0 + 16, :]
        return 0

    lax.fori_loop(0, NX, transposed, 0)

    def c_wait(k, _):
        j = lax.rem(i + k, NROW)
        rows = pl.ds(pl.multiple_of((j // NC) * 16, 16), 16)
        remote(c_send.at[j], carry.at[lax.rem(j, NC), rows], c_ss.at[j], c_rs.at[j], c, t).wait_recv()
        return 0

    lax.fori_loop(1, NROW, c_wait, 0)
    carry1 = [carry[k] for k in range(NC)]
    carry0 = [
        (bs1[:, k * 256:(k + 1) * 256] + jnp.exp(clos[1:2, k * 256:(k + 1) * 256]) * carry1[k].astype(F32)).astype(BF16)
        for k in range(NC)
    ]
    halo = remote(gc.at[pl.ds(0, 8)], gc.at[pl.ds(ROWS, 8)], h_ss, h_rs, prv, t)
    for n in range(NT):
        rows = slice(n * TILE, (n + 1) * TILE)
        for k in range(NC):
            lanes = slice(k * 256, (k + 1) * 256)
            beyond = dot(sin[rows, :], (carry0 if n < NT // 2 else carry1)[k], ((1,), (0,)))
            value = a_ref[rows, lanes] + b_ref[rows, lanes] * beyond
            gc[rows, lanes] = value.astype(BF16).astype(F32)
        if n == 0:
            halo.start()
    for name in ("taps", "vp"):
        loads[name].wait()
    for n in range(NT):
        r0 = n * TILE
        rows = slice(r0, r0 + TILE)
        if n == NT - 1:
            halo.wait_recv()
            gc[ROWS:ROWS + 8, :] = jnp.where(c == NCTX - 1, 0.0, gc[ROWS:ROWS + 8, :])
        summed = taps[0:1, :] * gc[r0 + 3:r0 + 3 + TILE, :]
        for j in range(1, 4):
            summed = summed + taps[j:j + 1, :] * gc[r0 + 3 - j:r0 + 3 - j + TILE, :]
        gp[rows, :] = summed.astype(BF16)
        for k in (1, 3, 2):
            tt = lax.rem(t + k, NX)
            part = dot(gp[rows, :], vp[pl.ds(pl.multiple_of(tt * FEAT, FEAT), FEAT), :], ((1,), (1,)))
            p_send[tt, rows, :] = part.astype(BF16)
            remote(p_send.at[tt, pl.ds(r0, TILE)], x_recv.at[t, pl.ds(r0, TILE)], x_ss.at[n, tt], x_rs.at[n, t], c, tt).start()

    other = 1 - core
    mate = c + 1 - 2 * core

    def w_copy(q):
        return remote(w_send.at[q], w_recv.at[q], w_ss.at[q], w_rs.at[q], mate, t)

    for q in range(Q):
        w_send[q] = dot(lt[other], gp[:, q * QW:(q + 1) * QW], ((1,), (0,))).astype(BF16)
        w_copy(q).start()
    for q in range(Q):
        w_own[q] = dot(lt[core], gp[:, q * QW:(q + 1) * QW], ((1,), (0,)))
    x_own[...] = dot(gp[...], vp[pl.ds(pl.multiple_of(t * FEAT, FEAT), FEAT), :], ((1,), (1,)))

    for q in range(Q):
        w_copy(q).wait_recv()
        for k in (2, 1, 3):
            yy = lax.rem(y + k, NY)
            rows = pl.ds(pl.multiple_of(yy * 128, 128), 128)
            v_send[q, yy] = (w_own[q, rows, :] + w_recv[q, rows, :].astype(F32)).astype(BF16)
            remote(v_send.at[q, yy], v_recv.at[q, y], v_ss.at[q, yy], v_rs.at[q, y], lax.rem(c + k * NROW, NCTX), t).start()
        rows = pl.ds(pl.multiple_of(y * 128, 128), 128)
        u_own[q] = w_own[q, rows, :] + w_recv[q, rows, :].astype(F32)
    for q in range(Q):
        acc = u_own[q]
        for k in range(1, NY):
            yy = lax.rem(y + k, NY)
            remote(v_send.at[q, yy], v_recv.at[q, yy], v_ss.at[q, yy], v_rs.at[q, yy], c, t).wait_recv()
            acc = acc + v_recv[q, yy].astype(F32)
        u_own[q] = acc
        u_send[q] = acc.astype(BF16)

        def u_start(k, _, q=q):
            zz = lax.rem(z + k, NZ)
            rows = pl.ds(pl.multiple_of(zz * 16, 16), 16)
            remote(u_send.at[q, rows], u_recv.at[q, z], u_ss.at[q, zz], u_rs.at[q, z], row0 + zz * NC + core, t).start()
            return 0

        lax.fori_loop(1, NZ, u_start, 0)

    for n in range(NT):
        rows = slice(n * TILE, (n + 1) * TILE)
        acc = x_own[rows, :]
        for k in range(1, NX):
            tt = lax.rem(t + k, NX)
            remote(p_send.at[tt, pl.ds(n * TILE, TILE)], x_recv.at[tt, pl.ds(n * TILE, TILE)], x_ss.at[n, tt], x_rs.at[n, tt], c, tt).wait_recv()
            acc = acc + x_recv[tt, rows, :].astype(F32)
        gi_ref[rows, :] = acc.astype(BF16)

    for q in range(Q):
        def u_add(k, acc, q=q):
            zz = lax.rem(z + k, NZ)
            remote(u_send.at[q, pl.ds(0, 16)], u_recv.at[q, zz], u_ss.at[q, zz], u_rs.at[q, zz], c, t).wait_recv()
            return acc + u_recv[q, zz].astype(F32)

        acc = lax.fori_loop(1, NZ, u_add, u_own[q, my_rows, :])
        gv_ref[:, q * QW:(q + 1) * QW] = acc * (1.0 / math.sqrt(ROWS * NCTX))

    def sent(k, _):
        d_copy(k).wait_send()
        s_copy(k).wait_send()
        c_copy(k).wait_send()
        return 0

    lax.fori_loop(1, NROW, sent, 0)
    for k in range(1, NX):
        tt = lax.rem(t + k, NX)
        remote(lay_h, lay.at[t], lay_ss.at[tt], lay_rs.at[t], c, tt).wait_send()
        for n in range(NT):
            part = pl.ds(n * TILE, TILE)
            remote(p_send.at[tt, part], x_recv.at[t, part], x_ss.at[n, tt], x_rs.at[n, t], c, tt).wait_send()
    halo.wait_send()
    for k in range(1, NY):
        yy = lax.rem(y + k, NY)
        remote(y_send, y_recv.at[y], y_ss.at[yy], y_rs.at[y], c, t).wait_send()
        for q in range(Q):
            remote(v_send.at[q, yy], v_recv.at[q, y], v_ss.at[q, yy], v_rs.at[q, y], c, t).wait_send()
    for q in range(Q):
        w_copy(q).wait_send()

        def u_sent(k, _, q=q):
            zz = lax.rem(z + k, NZ)
            remote(u_send.at[q, pl.ds(0, 16)], u_recv.at[q, z], u_ss.at[q, zz], u_rs.at[q, z], c, t).wait_send()
            return 0

        lax.fori_loop(1, NZ, u_sent, 0)


def local(layer_input, value_proj, conv_taps, conv_pre, state_in, state_out, step_size, log_decay, skip_gain, grad_out):
    dma = pltpu.SemaphoreType.DMA
    V = pltpu.VMEM
    scratch = [
        V((NX, ROWS, FEAT), BF16), V((NX * FEAT, CH), BF16), V((4, CH), F32), V((ROWS, CH), BF16),
        V((ROWS, STATE), BF16), V((ROWS, STATE), BF16), V((HEADS, ROWS), F32), V((HEADS, ROWS), F32),
        V((1, HEADS), F32), V((ROWS, CH), BF16),
        V((HEADS, ROWS), F32), V((ROWS, CH), F32), V((ROWS, CH), F32), V((ROWS + 8, CH), F32), V((ROWS, CH), BF16),
        V((STATE, CH), F32), V((8, CH), F32), V((NC, ROWS, ROWS), BF16),
        V((NC, STATE, 256), BF16), V((NROW, 16, 256), BF16), V((NC, 1, 256), F32), V((NROW, 1, 256), F32),
        V((NROW, 16, 256), F32), V((NROW, 1, 256), F32), V((24, 256), F32), V((NY, 24, 256), F32),
        V((NROW, 16, 256), BF16), V((NC, STATE, 256), BF16),
        V((NX, ROWS, FEAT), BF16), V((NX, ROWS, FEAT), BF16), V((ROWS, FEAT), F32),
        V((Q, 512, QW), BF16), V((Q, 512, QW), BF16), V((Q, 512, QW), F32),
        V((Q, NY, 128, QW), BF16), V((Q, NY, 128, QW), BF16), V((Q, 128, QW), F32),
        V((Q, 128, QW), BF16), V((Q, NZ, 16, QW), BF16),
        dma((10,)), dma((NX,)), dma((NX,)), dma((NROW,)), dma((NROW,)), dma((NROW,)), dma((NROW,)),
        dma((NY,)), dma((NY,)), dma((NROW,)), dma((NROW,)), dma, dma,
        dma((NT, NX)), dma((NT, NX)), dma((Q,)), dma((Q,)), dma((Q, NY)), dma((Q, NY)), dma((Q, NZ)), dma((Q, NZ)),
    ]
    return pl.pallas_call(
        kernel,
        out_shape=(
            jax.ShapeDtypeStruct((ROWS, FEAT), BF16),
            jax.ShapeDtypeStruct((16, CH), F32),
        ),
        in_specs=[pl.BlockSpec(memory_space=pl.ANY)] * 10,
        out_specs=(pl.BlockSpec(memory_space=pltpu.VMEM), pl.BlockSpec(memory_space=pltpu.VMEM)),
        scratch_shapes=scratch,
        compiler_params=pltpu.CompilerParams(
            collective_id=0, has_side_effects=True, vmem_limit_bytes=48 * 2**20
        ),
        cost_estimate=pl.CostEstimate(flops=1_500_000_000, bytes_accessed=4_000_000, transcendentals=2_000_000),
        name="scan_backward",
    )(
        layer_input, value_proj, conv_taps, conv_pre, state_in, state_out, step_size, log_decay,
        skip_gain.reshape(1, HEADS), grad_out,
    )


def solution(mesh):
    return jax.shard_map(
        local,
        mesh=mesh,
        in_specs=(
            P("context", "tensor"),
            P(None, "tensor"),
            P(None, "tensor"),
            P("context", "tensor"),
            P("context", None),
            P("context", None),
            P("tensor", "context"),
            P("tensor", "context"),
            P("tensor"),
            P("context", "tensor"),
        ),
        out_specs=(P("context", "tensor"), P("context", "tensor")),
        check_vma=False,
    )
```

time: 437 us -> 56.4 us (0.13); the launches traced: 430 us -> 56 us
  waiting for transfers between devices: 162 us -> 0 us
  blocking collectives: 129 us -> 0 us
  other arithmetic: 71.6 us -> 0 us
  Pallas kernels: 0 us -> 45.2 us
  local copies, waits for them, and re-layouts: 27.5 us -> 10.2 us
  matrix products: 14 us -> 0 us
  between operations: 14.6 us -> 0.66 us
  starting transfers between devices: 8.21 us -> 0 us
    unnamed x5 -> x0, waiting for transfers between devices: 139 us -> none
    unnamed x1 -> x0, blocking collectives: 129 us -> none
    add x64 -> x0, other arithmetic: 66 us -> none  [the longest x62 65.8 us: combine(): later_part[1] + jnp.exp(later_part[0])[:, None, None] * earlier_part[1]]
    pallas_call x0 -> x1, Pallas kernels: none -> 45.2 us  [local(): pl.pallas_call(kernel, out_shape=(jax.ShapeDtypeStruct((ROWS, FEAT), BF16...]
    reduce_scatter x1 -> x0, waiting for transfers between devices: 21.7 us -> none  [local(): lax.psum_scatter(partial_input, 'tensor', scatter_dimension=1, tiled=True)]
    dynamic_update_slice x4 -> x0, local copies, waits for them, and re-layouts: 15.6 us -> none  [local(): lax.scan(whole_increment, incoming, block_inputs, reverse=True)[1]]
    dot_general x9 -> x0, matrix products: 14 us -> none  [the longest x2 3.61 us: within_part(): jnp.einsum('hts,shp->thp', weights, grad_blk, preferred_element_type=jnp....]
    ppermute x1 -> x0, starting transfers between devices: 8.05 us -> none  [from_behind(): lax.ppermute(value, axis, [(source, source + steps) for source in range(l...]
  transfers between devices with their start and end apart: 5 -> 0, of which waited for: 3 -> 0; matrix products, arithmetic and copies ran while one was open for 24% -> 0% of each run, Pallas kernels for 0% -> 0%
where the time goes in v1:
time: 56.4 us; the launch traced here: 56 us
  Pallas kernels  45.2 us (80%)
  local copies, waits for them, and re-layouts  10.2 us (18%)
  between operations  0.66 us (1%)
    pallas_call x1, Pallas kernels, local(): pl.pallas_call(kernel, out_shape=(jax.ShapeDtypeStruct((ROWS, FEAT), BF16...  45.2 us
    unnamed x22, local copies, waits for them, and re-layouts  10.2 us

profile of v1, /device:TPU:1, one launch (start us, length us, event | category | flops | bytes accessed | tf_op | source)
XLA Modules:
  0.0 56.0 jit_solution(8593754552230627357)
XLA Ops:
  0.6 0.0 copy-start.9
  0.6 0.6 %copy-done.9 = f32[8]{0:T(128)S(1)} copy-done((f32[8]{0:T(128)S(1)}, f32[8]{0:T(128)}, u32[]{:S(2)}) %copy-start.9) | copy-done | bytes 56
  1.3 0.0 copy-start
  1.3 1.2 %copy-done = bf16[1024,512]{1,0:T(8,128)(2,1)S(1)} copy-done((bf16[1024,512]{1,0:T(8,128)(2,1)S(1)}, bf16[1024,512]{1,0:T(8,128)(2,1)}, u32[]{:S(2)}) %copy-start) | copy-done | bytes 1048600
  2.5 0.0 copy-start.1
  2.5 1.0 %copy-done.1 = bf16[512,512]{1,0:T(8,128)(2,1)S(1)} copy-done((bf16[512,512]{1,0:T(8,128)(2,1)S(1)}, bf16[512,512]{1,0:T(8,128)(2,1)}, u32[]{:S(2)}) %copy-start.1) | copy-done | bytes 524312
  3.6 0.0 copy-start.2
  3.6 1.0 %copy-done.2 = bf16[512,512]{1,0:T(8,128)(2,1)S(1)} copy-done((bf16[512,512]{1,0:T(8,128)(2,1)S(1)}, bf16[512,512]{1,0:T(8,128)(2,1)}, u32[]{:S(2)}) %copy-start.2) | copy-done | bytes 524312
  4.6 0.0 copy-start.3
  4.6 0.9 %copy-done.3 = bf16[512,256]{1,0:T(8,128)(2,1)S(1)} copy-done((bf16[512,256]{1,0:T(8,128)(2,1)S(1)}, bf16[512,256]{1,0:T(8,128)(2,1)}, u32[]{:S(2)}) %copy-start.3) | copy-done | bytes 262168
  5.5 0.0 copy-start.4
  5.6 0.9 %copy-done.4 = bf16[512,128]{1,0:T(8,128)(2,1)S(1)} copy-done((bf16[512,128]{1,0:T(8,128)(2,1)S(1)}, bf16[512,128]{1,0:T(8,128)(2,1)}, u32[]{:S(2)}) %copy-start.4) | copy-done | bytes 131096
  6.5 0.0 copy-start.5
  6.5 0.9 %copy-done.5 = bf16[512,128]{1,0:T(8,128)(2,1)S(1)} copy-done((bf16[512,128]{1,0:T(8,128)(2,1)S(1)}, bf16[512,128]{1,0:T(8,128)(2,1)}, u32[]{:S(2)}) %copy-start.5) | copy-done | bytes 131096
  7.4 0.0 copy-start.6
  7.4 0.7 %copy-done.6 = f32[8,512]{1,0:T(8,128)S(1)} copy-done((f32[8,512]{1,0:T(8,128)S(1)}, f32[8,512]{1,0:T(8,128)}, u32[]{:S(2)}) %copy-start.6) | copy-done | bytes 16408
  8.1 0.0 copy-start.7
  8.1 0.7 %copy-done.7 = f32[8,512]{1,0:T(8,128)S(1)} copy-done((f32[8,512]{1,0:T(8,128)S(1)}, f32[8,512]{1,0:T(8,128)}, u32[]{:S(2)}) %copy-start.7) | copy-done | bytes 16408
  8.8 0.0 copy-start.8
  8.8 0.7 %copy-done.8 = f32[4,512]{1,0:T(4,128)S(1)} copy-done((f32[4,512]{1,0:T(4,128)S(1)}, f32[4,512]{1,0:T(4,128)}, u32[]{:S(2)}) %copy-start.8) | copy-done | bytes 8216
  9.5 45.2 %scan_backward.1 = (bf16[512,256]{1,0:T(8,128)(2,1)S(1)}, f32[16,512]{1,0:T(8,128)S(1)}) custom-call(bf16[512,256]{1,0:T(8,128)(2,1)S(1)} %copy-done.3, bf16[1024,512]{1,0:T(8,128)(2,1)S(1)} %copy-done, f32[4,512]{1,0:T(4,128)S(1)} %copy-done.8, bf16[512,512]{1,0:T(8,128)(2,1)S(1)} %copy-done.1, bf16[512,128]{1,0:T(8,128)(2,1)S(1)} %copy-done.4, ...), custom_call_target="tpu_custom_call" | custom-call | flops 1500000000 | bytes 4000000 | tf_op jit(solution)/shard_map/scan_backward/pallas_call | solution.py:403
  54.7 0.7 %copy.14 = bf16[512,256]{1,0:T(8,128)(2,1)} copy(bf16[512,256]{1,0:T(8,128)(2,1)S(1)} %get-tuple-element.4) | data formatting | bytes 524288
  55.4 0.6 %copy.15 = f32[16,512]{1,0:T(8,128)} copy(f32[16,512]{1,0:T(8,128)S(1)} %get-tuple-element.5) | data formatting | bytes 65536
Async XLA Ops:
  0.6 0.7 %copy-start.9 = (f32[8]{0:T(128)S(1)}, f32[8]{0:T(128)}, u32[]{:S(2)}) copy-start(f32[8]{0:T(128)} %param.18) | copy-start | bytes 100
  1.3 1.2 %copy-start = (bf16[1024,512]{1,0:T(8,128)(2,1)S(1)}, bf16[1024,512]{1,0:T(8,128)(2,1)}, u32[]{:S(2)}) copy-start(bf16[1024,512]{1,0:T(8,128)(2,1)} %vp_h.1) | copy-start | bytes 3145732
  2.5 1.0 %copy-start.1 = (bf16[512,512]{1,0:T(8,128)(2,1)S(1)}, bf16[512,512]{1,0:T(8,128)(2,1)}, u32[]{:S(2)}) copy-start(bf16[512,512]{1,0:T(8,128)(2,1)} %pre_h.1) | copy-start | bytes 1572868
  3.6 1.0 %copy-start.2 = (bf16[512,512]{1,0:T(8,128)(2,1)S(1)}, bf16[512,512]{1,0:T(8,128)(2,1)}, u32[]{:S(2)}) copy-start(bf16[512,512]{1,0:T(8,128)(2,1)} %go_h.1) | copy-start | bytes 1572868
  4.6 0.9 %copy-start.3 = (bf16[512,256]{1,0:T(8,128)(2,1)S(1)}, bf16[512,256]{1,0:T(8,128)(2,1)}, u32[]{:S(2)}) copy-start(bf16[512,256]{1,0:T(8,128)(2,1)} %lay_h.1) | copy-start | bytes 786436
  5.5 0.9 %copy-start.4 = (bf16[512,128]{1,0:T(8,128)(2,1)S(1)}, bf16[512,128]{1,0:T(8,128)(2,1)}, u32[]{:S(2)}) copy-start(bf16[512,128]{1,0:T(8,128)(2,1)} %sin_h.1) | copy-start | bytes 393220
  6.5 0.9 %copy-start.5 = (bf16[512,128]{1,0:T(8,128)(2,1)S(1)}, bf16[512,128]{1,0:T(8,128)(2,1)}, u32[]{:S(2)}) copy-start(bf16[512,128]{1,0:T(8,128)(2,1)} %sout_h.1) | copy-start | bytes 393220
  7.4 0.7 %copy-start.6 = (f32[8,512]{1,0:T(8,128)S(1)}, f32[8,512]{1,0:T(8,128)}, u32[]{:S(2)}) copy-start(f32[8,512]{1,0:T(8,128)} %step_h.1) | copy-start | bytes 49156
  8.1 0.7 %copy-start.7 = (f32[8,512]{1,0:T(8,128)S(1)}, f32[8,512]{1,0:T(8,128)}, u32[]{:S(2)}) copy-start(f32[8,512]{1,0:T(8,128)} %ld_h.1) | copy-start | bytes 49156
  8.8 0.7 %copy-start.8 = (f32[4,512]{1,0:T(4,128)S(1)}, f32[4,512]{1,0:T(4,128)}, u32[]{:S(2)}) copy-start(f32[4,512]{1,0:T(4,128)} %taps_h.1) | copy-start | bytes 24580

commit v2 on v1

v2 whole, which is shorter than its diff:
```python
import functools
import math

import jax
import jax.numpy as jnp
from jax import lax
from jax.experimental import pallas as pl
from jax.experimental.pallas import tpu as pltpu
from jax.sharding import PartitionSpec as P

MESH = pl.DeviceIdType.MESH
F32, BF16 = jnp.float32, jnp.bfloat16
HIGH = lax.Precision.HIGHEST

NX, NY, NZ, NC = 4, 4, 8, 2
NROW = NZ * NC
NCTX = NY * NROW
ROWS, CH, STATE, BLOCK, HEADS, HD = 512, 512, 128, 256, 8, 64
FEAT, HALF = 256, 128
Q, QW = 2, 256
TILE, NT = 128, 4
XT, XR = 2, 256


def dot(a, b, dims, precision=None):
    return lax.dot_general(a, b, (dims, ((), ())), precision=precision, preferred_element_type=F32)


def remote(src, dst, send, recv, ctx, ten):
    return pltpu.make_async_remote_copy(
        src_ref=src, dst_ref=dst, send_sem=send, recv_sem=recv,
        device_id=(ctx, ten), device_id_type=MESH,
    )


def kernel(
    lay_h, vp_h, taps_h, pre_h, sin_h, sout_h, step_h, ld_h, skip_h, go_h,
    gi_ref, gv_ref,
    lay, vp, taps, pre, sin, sout, step, ld, skip, go,
    cum, a_ref, b_ref, gc, gp, bs1, clos, lt,
    s_send, s_recv, later, z_send, z_recv, rsuf, lsuf, y_send, y_recv, c_send, c_recv, m_send, carry,
    xo_send, xo_recv, xd_send, xd_recv, x_keep, x_own,
    w_send, w_recv, w_own, vo_send, vo_recv, vd_send, vd_recv, v_keep, u_own, u_send, u_recv,
    in_sem, lay_ss, lay_rs, s_ss, s_rs, z_ss, z_rs, y_ss, y_rs, c_ss, c_rs, m_ss, m_rs, h_ss, h_rs,
    xo_ss, xo_rs, xd_ss, xd_rs, w_ss, w_rs, vo_ss, vo_rs, vd_ss, vd_rs, u_ss, u_rs,
):
    c = lax.axis_index("context")
    t = lax.axis_index("tensor")
    core = lax.rem(c, NC)
    other = 1 - core
    z = lax.rem(c // NC, NZ)
    y = c // NROW
    row0 = y * NROW + core
    nxt, prv = lax.rem(c + 1, NCTX), lax.rem(c + NCTX - 1, NCTX)
    mate = c + 1 - 2 * core
    xs = [lax.rem(t + k, NX) for k in range(NX)]
    ys = [lax.rem(y + k, NY) for k in range(NY)]
    yc = [lax.rem(c + k * NROW, NCTX) for k in range(NY)]
    zs = [lax.rem(z + k, NZ) for k in range(NZ)]
    zc = [row0 + k * NC for k in zs]

    def slab(k, n):
        return pl.ds(pl.multiple_of(k * n, n), n)

    barrier = pltpu.get_barrier_semaphore()
    partners = [(zc[k], t) for k in range(1, NZ)] + [(yc[k], t) for k in range(1, NY)]
    partners += [(c, xs[1]), (c, xs[3]), (nxt, t), (prv, t)]
    for ctx, ten in partners:
        pl.semaphore_signal(barrier, inc=1, device_id=(ctx, ten), device_id_type=MESH)

    loads = {}
    for n, (name, src, dst) in enumerate((
        ("ld", ld_h, ld), ("go", go_h, go), ("sout", sout_h, sout), ("sin", sin_h, sin),
        ("step", step_h, step), ("skip", skip_h, skip), ("pre", pre_h, pre), ("taps", taps_h, taps),
        ("vp", vp_h, vp), ("lay", lay_h, lay.at[t]),
    )):
        loads[name] = pltpu.make_async_copy(src, dst, in_sem.at[n])
        loads[name].start()

    ri = lax.broadcasted_iota(jnp.int32, (BLOCK, BLOCK), 0)
    ci = lax.broadcasted_iota(jnp.int32, (BLOCK, BLOCK), 1)
    upto = (ri <= ci).astype(F32)
    hi = lax.broadcasted_iota(jnp.int32, (HEADS, CH), 0)
    li = lax.broadcasted_iota(jnp.int32, (HEADS, CH), 1)
    onehot = (li // HD == hi).astype(F32)
    loads["ld"].wait()
    for k in range(2):
        cum[:, k * BLOCK:(k + 1) * BLOCK] = dot(ld[:, k * BLOCK:(k + 1) * BLOCK], upto, ((1,), (0,)), HIGH)
    for k in range(2):
        b_ref[k * BLOCK:(k + 1) * BLOCK, :] = dot(cum[:, k * BLOCK:(k + 1) * BLOCK], onehot, ((0,), (0,)), HIGH)
    clos0 = b_ref[BLOCK - 1:BLOCK, :]
    clos1 = b_ref[2 * BLOCK - 1:2 * BLOCK, :]
    clos[0:1, :] = clos0
    clos[1:2, :] = clos1
    for k in range(NC):
        s_send[k, STATE:STATE + 8, :] = jnp.broadcast_to((clos0 + clos1)[:, k * 256:(k + 1) * 256], (8, 256))

    loads["go"].wait()
    loads["sout"].wait()
    state = None
    for k in range(2):
        w = (go[k * BLOCK:(k + 1) * BLOCK, :].astype(F32) * jnp.exp(b_ref[k * BLOCK:(k + 1) * BLOCK, :])).astype(BF16)
        bs = dot(sout[k * BLOCK:(k + 1) * BLOCK, :], w, ((0,), (0,)))
        if k == 0:
            state = bs
        else:
            bs1[...] = bs
            state = state + jnp.exp(clos0) * bs
    for k in range(NC):
        s_send[k, 0:STATE, :] = state[:, k * 256:(k + 1) * 256]

    pl.semaphore_wait(barrier, len(partners))

    s_copy = remote(s_send.at[other], s_recv, s_ss, s_rs, mate, t)
    s_copy.start()

    remote(lay_h, lay.at[t], lay_ss.at[0], lay_rs.at[0], c, xs[1]).start()
    remote(lay_h, lay.at[t], lay_ss.at[1], lay_rs.at[1], c, xs[3]).start()

    def within(k):
        rows = slice(k * BLOCK, (k + 1) * BLOCK)
        scores = dot(sin[rows, :], sout[rows, :], ((1,), (1,)))
        scores = jnp.where(ci >= ri, scores, 0.0)
        low = lax.broadcasted_iota(jnp.int32, (BLOCK, 128), 1) < HD
        cum_t = cum[:, rows].T
        for pair in range(HEADS // 2):
            lanes = slice(pair * 128, pair * 128 + 128)
            g = go[rows, lanes]
            parts = []
            for h in (2 * pair, 2 * pair + 1):
                spread = cum[h:h + 1, rows] - cum_t[:, h:h + 1]
                weights = (scores * jnp.exp(jnp.minimum(spread, 0.0))).astype(BF16)
                parts.append(dot(weights, g, ((1,), (0,))))
            a_ref[rows, lanes] = jnp.where(low, parts[0], parts[1])

    loads["sin"].wait()
    within(0)

    s_copy.wait_recv()
    first = jnp.where(core == 0, s_send[core], s_recv[...])
    second = jnp.where(core == 0, s_recv[...], s_send[core])
    later[...] = second
    d_first, d_second = first[STATE:STATE + 1, :], second[STATE:STATE + 1, :]
    chip = first[0:STATE, :] + jnp.exp(d_first) * second[0:STATE, :]
    z_send[:, 0:256] = chip.astype(BF16)
    d_chip = d_first + d_second
    row = lax.broadcasted_iota(jnp.int32, (16, 128), 0)
    extra = jnp.zeros((16, 128), F32)
    rest = d_chip
    for n in range(3):
        piece = rest.astype(BF16).astype(F32)
        rest = rest - piece
        extra = jnp.where(row == 2 * n, piece[:, 0:128], extra)
        extra = jnp.where(row == 2 * n + 1, piece[:, 128:256], extra)
    extra = extra.astype(BF16)
    for n in range(NZ):
        z_send[n * 16:(n + 1) * 16, 256:384] = extra
    for k in (4, 3, 5, 2, 6, 1, 7):
        remote(z_send.at[slab(zs[k], 16)], z_recv.at[z], z_ss, z_rs, zc[k], t).start()
    z_recv[z] = z_send[slab(z, 16), :]

    within(1)

    remote(z_send.at[pl.ds(0, 112)], z_recv.at[pl.ds(0, NZ - 1)], z_ss, z_rs, c, t).wait_recv()
    r, l = jnp.zeros((16, 256), F32), jnp.zeros((1, 256), F32)
    for j in range(NZ - 1, -1, -1):
        rsuf[j] = r
        lsuf[j] = l
        got = z_recv[j].astype(F32)
        d = jnp.concatenate(
            [got[n:n + 1, 256:384] + got[n + 2:n + 3, 256:384] + got[n + 4:n + 5, 256:384] for n in range(2)], axis=1
        )
        r, l = got[:, 0:256] + jnp.exp(d) * r, l + d
    y_send[0:16, :] = r
    y_send[16:24, :] = jnp.broadcast_to(l, (8, 256))
    for k in (2, 1, 3):
        remote(y_send, y_recv.at[y], y_ss, y_rs, yc[k], t).start()
    y_recv[y] = y_send[...]

    for k, n in ((3, 0), (1, 1)):
        remote(lay_h, lay.at[xs[k]], lay_ss.at[n], lay_rs.at[n], c, t).wait_recv()
        half = pl.ds(n * 256, 256)
        block = lay.at[xs[k], half]
        remote(block, block, lay_ss.at[2 + n], lay_rs.at[2 + n], c, xs[4 - k]).start()

    for name in ("step", "skip", "pre"):
        loads[name].wait()
    skip_e = dot(skip[...], onehot, ((1,), (0,)), HIGH)

    def factors(n):
        rows = slice(n * 64, (n + 1) * 64)
        close = clos[n // 4:n // 4 + 1, :]
        v = pre[rows, :].astype(F32)
        sig = 1.0 / (1.0 + jnp.exp(-v))
        slope = sig * (1.0 + v * (1.0 - sig))
        step_e = dot(step[:, rows], onehot, ((0,), (0,)), HIGH)
        a_ref[rows, :] = (step_e * a_ref[rows, :] + skip_e * go[rows, :].astype(F32)) * slope
        b_ref[rows, :] = step_e * jnp.exp(close - b_ref[rows, :]) * slope

    for n in range(4):
        factors(n)

    remote(y_send, y_recv.at[pl.ds(0, NY - 1)], y_ss, y_rs, c, t).wait_recv()
    coming = jnp.zeros((16, 256), F32)
    for yy in range(NY - 1, 0, -1):
        r = y_recv[yy]
        coming = jnp.where(yy > y, r[0:16, :] + jnp.exp(r[16:17, :]) * coming, coming)
    for j in range(NZ):
        c_send[j * 16:(j + 1) * 16, :] = (rsuf[j] + jnp.exp(lsuf[j]) * coming).astype(BF16)
    for k in (4, 3, 5, 2, 6, 1, 7):
        remote(c_send.at[slab(zs[k], 16)], c_recv.at[slab(z, 16)], c_ss, c_rs, zc[k], t).start()
    c_recv[slab(z, 16), :] = c_send[slab(z, 16), :]

    for n in range(4, 8):
        factors(n)

    def transposed(x):
        for half in range(2):
            cols = slice(half * 256, half * 256 + 256)
            tr = lay[x, cols, :].T
            for zz in range(NZ):
                for cc in range(NC):
                    f0 = (zz * NC + cc) * 16
                    lt[cc, pl.ds(pl.multiple_of(x * 128 + zz * 16, 16), 16), cols] = tr[f0:f0 + 16, :]

    loads["lay"].wait()
    for k in (0, 1, 3):
        transposed(xs[k])

    remote(c_send, c_recv.at[pl.ds(0, 112)], c_ss, c_rs, c, t).wait_recv()
    into_second = c_recv[...]
    into_first = (later[0:STATE, :] + jnp.exp(later[STATE:STATE + 1, :]) * into_second.astype(F32)).astype(BF16)
    m_send[...] = jnp.where(core == 0, into_second, into_first)
    m_copy = remote(m_send, carry.at[core], m_ss, m_rs, mate, t)
    m_copy.start()
    carry[core] = jnp.where(core == 0, into_first, into_second)

    for n, rows in ((0, pl.ds(0, 256)), (1, pl.ds(256, 256))):
        block = lay.at[xs[2], rows]
        remote(block, block, lay_ss.at[2 + n], lay_rs.at[2 + n], c, t).wait_recv()
    transposed(xs[2])
    for name in ("taps", "vp"):
        loads[name].wait()

    remote(m_send, carry.at[other], m_ss, m_rs, mate, t).wait_recv()
    carry1 = [carry[k] for k in range(NC)]
    carry0 = [
        (bs1[:, k * 256:(k + 1) * 256] + jnp.exp(clos[1:2, k * 256:(k + 1) * 256]) * carry1[k].astype(F32)).astype(BF16)
        for k in range(NC)
    ]
    halo = remote(gc.at[pl.ds(0, 8)], gc.at[pl.ds(ROWS, 8)], h_ss, h_rs, prv, t)
    for n in range(NT):
        rows = slice(n * TILE, (n + 1) * TILE)
        for k in range(NC):
            lanes = slice(k * 256, (k + 1) * 256)
            beyond = dot(sin[rows, :], (carry0 if n < NT // 2 else carry1)[k], ((1,), (0,)))
            value = a_ref[rows, lanes] + b_ref[rows, lanes] * beyond
            gc[rows, lanes] = value.astype(BF16).astype(F32)
        if n == 0:
            halo.start()

    def weights_of(k):
        return vp[slab(xs[k], FEAT), :]

    for n in range(XT):
        rows = slice(n * XR, (n + 1) * XR)
        for r0 in range(n * XR, (n + 1) * XR, TILE):
            if r0 == ROWS - TILE:
                halo.wait_recv()
                gc[ROWS:ROWS + 8, :] = jnp.where(c == NCTX - 1, 0.0, gc[ROWS:ROWS + 8, :])
            summed = taps[0:1, :] * gc[r0 + 3:r0 + 3 + TILE, :]
            for j in range(1, 4):
                summed = summed + taps[j:j + 1, :] * gc[r0 + 3 - j:r0 + 3 - j + TILE, :]
            gp[r0:r0 + TILE, :] = summed.astype(BF16)
        part = dot(gp[rows, :], weights_of(2), ((1,), (1,)))
        for s in range(2):
            xo_send[n, s] = part[:, s * HALF:(s + 1) * HALF].astype(BF16)
            remote(xo_send.at[n, s], xo_recv.at[n, s], xo_ss, xo_rs.at[n, s], c, xs[(1, 3)[s]]).start()

    def w_copy(q):
        return remote(w_send.at[q], w_recv.at[q], w_ss.at[q], w_rs.at[q], mate, t)

    for q in range(Q):
        w_send[q] = dot(lt[other], gp[:, q * QW:(q + 1) * QW], ((1,), (0,))).astype(BF16)
        w_copy(q).start()

    def xd_start(n, s, half):
        remote(xd_send.at[n, s, half], xd_recv.at[n, s, half], xd_ss, xd_rs.at[n, s, half], c, xs[(1, 3)[s]]).start()

    for n in range(XT):
        rows = slice(n * XR, (n + 1) * XR)
        for s in range(2):
            part = dot(gp[rows, :], weights_of((1, 3)[s]), ((1,), (1,)))
            xd_send[n, s, 1 - s] = part[:, (1 - s) * HALF:(2 - s) * HALF].astype(BF16)
            xd_start(n, s, 1 - s)
            x_keep[n, s] = part[:, s * HALF:(s + 1) * HALF]

    for q in range(Q):
        w_own[q] = dot(lt[core], gp[:, q * QW:(q + 1) * QW], ((1,), (0,)))

    def vd_start(q, s, half):
        remote(vd_send.at[q, s, half], vd_recv.at[q, s, half], vd_ss, vd_rs.at[q, s, half], yc[(1, 3)[s]], t).start()

    for q in range(Q):
        w_copy(q).wait_recv()

        def both(k, q=q):
            rows = slab(ys[k], 128)
            return w_own[q, rows, :] + w_recv[q, rows, :].astype(F32)

        part = both(2)
        for s in range(2):
            vo_send[q, s] = part[:, s * HALF:(s + 1) * HALF].astype(BF16)
            remote(vo_send.at[q, s], vo_recv.at[q, s], vo_ss, vo_rs.at[q, s], yc[(1, 3)[s]], t).start()
        for s in range(2):
            part = both((1, 3)[s])
            vd_send[q, s, 1 - s] = part[:, (1 - s) * HALF:(2 - s) * HALF].astype(BF16)
            vd_start(q, s, 1 - s)
            v_keep[q, s] = part[:, s * HALF:(s + 1) * HALF]
        u_own[:, q * QW:(q + 1) * QW] = both(0)

    x_own[...] = dot(gp[...], weights_of(0), ((1,), (1,)))

    def x_relay(n):
        for s in range(2):
            remote(xo_send.at[n, s], xo_recv.at[n, s], xo_ss, xo_rs.at[n, s], c, t).wait_recv()
            xd_send[n, s, s] = (x_keep[n, s] + xo_recv[n, s].astype(F32)).astype(BF16)
            xd_start(n, s, s)

    def v_relay(q):
        for s in range(2):
            remote(vo_send.at[q, s], vo_recv.at[q, s], vo_ss, vo_rs.at[q, s], c, t).wait_recv()
            vd_send[q, s, s] = (v_keep[q, s] + vo_recv[q, s].astype(F32)).astype(BF16)
            vd_start(q, s, s)

    x_relay(0)
    v_relay(0)
    x_relay(1)
    v_relay(1)

    for q in range(Q):
        for half in range(2):
            lanes = slice(q * QW + half * HALF, q * QW + (half + 1) * HALF)
            acc = u_own[:, lanes]
            for s in range(2):
                remote(vd_send.at[q, s, half], vd_recv.at[q, s, half], vd_ss, vd_rs.at[q, s, half], c, t).wait_recv()
                acc = acc + vd_recv[q, s, half].astype(F32)
            u_own[:, lanes] = acc
            u_send[:, lanes] = acc.astype(BF16)
    for k in (4, 3, 5, 2, 6, 1, 7):
        remote(u_send.at[slab(zs[k], 16)], u_recv.at[z], u_ss, u_rs, zc[k], t).start()
    u_recv[z] = jnp.zeros((16, CH), BF16)

    for n in range(XT):
        rows = slice(n * XR, (n + 1) * XR)
        for half in range(2):
            lanes = slice(half * HALF, (half + 1) * HALF)
            acc = x_own[rows, lanes]
            for s in range(2):
                remote(xd_send.at[n, s, half], xd_recv.at[n, s, half], xd_ss, xd_rs.at[n, s, half], c, t).wait_recv()
                acc = acc + xd_recv[n, s, half].astype(F32)
            gi_ref[rows, lanes] = acc.astype(BF16)

    remote(u_send.at[pl.ds(0, 112)], u_recv.at[pl.ds(0, NZ - 1)], u_ss, u_rs, c, t).wait_recv()
    acc = u_own[slab(z, 16), :]
    for k in range(NZ):
        acc = acc + u_recv[k].astype(F32)
    gv_ref[...] = acc * (1.0 / math.sqrt(ROWS * NCTX))

    def sent(src, sem):
        remote(src, src, sem, h_rs, c, t).wait_send()

    sent(s_send.at[other], s_ss)
    sent(lay_h, lay_ss.at[0])
    sent(lay_h, lay_ss.at[1])
    sent(lay.at[0, pl.ds(0, 256)], lay_ss.at[2])
    sent(lay.at[0, pl.ds(0, 256)], lay_ss.at[3])
    sent(z_send.at[pl.ds(0, 112)], z_ss)
    sent(y_recv.at[pl.ds(0, NY - 1)], y_ss)
    sent(c_send.at[pl.ds(0, 112)], c_ss)
    sent(m_send, m_ss)
    sent(gc.at[pl.ds(0, 8)], h_ss)
    sent(xo_send, xo_ss)
    sent(xd_send, xd_ss)
    for q in range(Q):
        w_copy(q).wait_send()
    sent(vo_send, vo_ss)
    sent(vd_send, vd_ss)
    sent(u_send.at[pl.ds(0, 112)], u_ss)


def place(gi, gv, gi_out, gv_out, sem):
    copies = [pltpu.make_async_copy(gi, gi_out, sem.at[0]), pltpu.make_async_copy(gv, gv_out, sem.at[1])]
    for copy in copies:
        copy.start()
    for copy in copies:
        copy.wait()


def local(layer_input, value_proj, conv_taps, conv_pre, state_in, state_out, step_size, log_decay, skip_gain, grad_out):
    dma = pltpu.SemaphoreType.DMA
    V = pltpu.VMEM
    scratch = [
        V((NX, ROWS, FEAT), BF16), V((NX * FEAT, CH), BF16), V((4, CH), F32), V((ROWS, CH), BF16),
        V((ROWS, STATE), BF16), V((ROWS, STATE), BF16), V((HEADS, ROWS), F32), V((HEADS, ROWS), F32),
        V((1, HEADS), F32), V((ROWS, CH), BF16),
        V((HEADS, ROWS), F32), V((ROWS, CH), F32), V((ROWS, CH), F32), V((ROWS + 8, CH), F32), V((ROWS, CH), BF16),
        V((STATE, CH), F32), V((8, CH), F32), V((NC, ROWS, ROWS), BF16),
        V((NC, STATE + 8, 256), F32), V((STATE + 8, 256), F32), V((STATE + 8, 256), F32),
        V((STATE, 384), BF16), V((NZ, 16, 384), BF16), V((NZ, 16, 256), F32), V((NZ, 1, 256), F32),
        V((24, 256), F32), V((NY, 24, 256), F32),
        V((STATE, 256), BF16), V((STATE, 256), BF16), V((STATE, 256), BF16), V((NC, STATE, 256), BF16),
        V((XT, 2, XR, HALF), BF16), V((XT, 2, XR, HALF), BF16), V((XT, 2, 2, XR, HALF), BF16), V((XT, 2, 2, XR, HALF), BF16),
        V((XT, 2, XR, HALF), F32), V((ROWS, FEAT), F32),
        V((Q, 512, QW), BF16), V((Q, 512, QW), BF16), V((Q, 512, QW), F32),
        V((Q, 2, 128, HALF), BF16), V((Q, 2, 128, HALF), BF16), V((Q, 2, 2, 128, HALF), BF16), V((Q, 2, 2, 128, HALF), BF16),
        V((Q, 2, 128, HALF), F32), V((128, CH), F32), V((128, CH), BF16), V((NZ, 16, CH), BF16),
        dma((10,)), dma((4,)), dma((4,)), dma, dma, dma, dma, dma, dma, dma, dma, dma, dma, dma, dma,
        dma, dma((XT, 2)), dma, dma((XT, 2, 2)), dma((Q,)), dma((Q,)), dma, dma((Q, 2)), dma, dma((Q, 2, 2)), dma, dma,
    ]
    outs = (jax.ShapeDtypeStruct((ROWS, FEAT), BF16), jax.ShapeDtypeStruct((16, CH), F32))
    gi, gv = pl.pallas_call(
        kernel,
        out_shape=outs,
        in_specs=[pl.BlockSpec(memory_space=pl.ANY)] * 10,
        out_specs=(pl.BlockSpec(memory_space=pltpu.VMEM), pl.BlockSpec(memory_space=pltpu.VMEM)),
        scratch_shapes=scratch,
        compiler_params=pltpu.CompilerParams(
            collective_id=0, has_side_effects=True, vmem_limit_bytes=60 * 2**20
        ),
        cost_estimate=pl.CostEstimate(flops=1_500_000_000, bytes_accessed=4_000_000, transcendentals=2_000_000),
        name="scan_backward",
    )(
        layer_input, value_proj, conv_taps, conv_pre, state_in, state_out, step_size, log_decay,
        skip_gain.reshape(1, HEADS), grad_out,
    )
    return pl.pallas_call(
        place,
        out_shape=outs,
        in_specs=[pl.BlockSpec(memory_space=pl.ANY)] * 2,
        out_specs=(pl.BlockSpec(memory_space=pl.ANY), pl.BlockSpec(memory_space=pl.ANY)),
        scratch_shapes=[dma((2,))],
        name="place_outputs",
    )(gi, gv)


def solution(mesh):
    return jax.shard_map(
        local,
        mesh=mesh,
        in_specs=(
            P("context", "tensor"),
            P(None, "tensor"),
            P(None, "tensor"),
            P("context", "tensor"),
            P("context", None),
            P("context", None),
            P("tensor", "context"),
            P("tensor", "context"),
            P("tensor"),
            P("context", "tensor"),
        ),
        out_specs=(P("context", "tensor"), P("context", "tensor")),
        check_vma=False,
    )
```

time: 56.4 us -> 54.5 us (0.966)
  local copies, waits for them, and re-layouts: 10.2 us -> 0 us
  Pallas kernels: 45.2 us -> 53.8 us
    unnamed x22 -> x0, local copies, waits for them, and re-layouts: 10.2 us -> none
    pallas_call x1 -> x2, Pallas kernels: 45.2 us -> 53.8 us  [the longest x1 43.7 us: local(): pl.pallas_call(kernel, out_shape=outs, in_specs=[pl.BlockSpec(memory_spac...]
where the time goes in v2:
time: 54.5 us; the launch traced here: 54.4 us
  Pallas kernels  53.8 us (99%)
  between operations  0.64 us (1%)
    pallas_call x1, Pallas kernels, local(): pl.pallas_call(kernel, out_shape=outs, in_specs=[pl.BlockSpec(memory_spac...  43.7 us
    pallas_call x1, Pallas kernels, local(): pl.pallas_call(place, out_shape=outs, in_specs=[pl.BlockSpec(memory_space...  10.1 us

profile of v2, /device:TPU:1, one launch (start us, length us, event | category | flops | bytes accessed | tf_op | source)
XLA Modules:
  0.0 54.4 jit_solution(13438726281762603202)
XLA Ops:
  0.6 43.7 %scan_backward.1 = (bf16[512,256]{1,0:T(8,128)(2,1)}, f32[16,512]{1,0:T(8,128)}) custom-call(bf16[512,256]{1,0:T(8,128)(2,1)} %lay_h.1, bf16[1024,512]{1,0:T(8,128)(2,1)} %vp_h.1, f32[4,512]{1,0:T(4,128)} %taps_h.1, bf16[512,512]{1,0:T(8,128)(2,1)} %pre_h.1, bf16[512,128]{1,0:T(8,128)(2,1)} %sin_h.1, bf16[512,128]{1,0:T(8,128)(2,1)} %sout_h.1, ...), custom_call_target="tpu_custom_call" | custom-call | flops 1500000000 | bytes 4000000 | tf_op jit(solution)/shard_map/scan_backward/pallas_call | solution.py:422
  44.3 10.1 %place_outputs.1 = (bf16[512,256]{1,0:T(8,128)(2,1)}, f32[16,512]{1,0:T(8,128)}) custom-call(bf16[512,256]{1,0:T(8,128)(2,1)} %get-tuple-element.4.gi, f32[16,512]{1,0:T(8,128)} %get-tuple-element.5.gv), custom_call_target="tpu_custom_call" | custom-call | tf_op jit(solution)/shard_map/place_outputs/pallas_call | solution.py:437

commit v3 on v2

v3 whole, which is shorter than its diff:
```python
import functools
import math

import jax
import jax.numpy as jnp
from jax import lax
from jax.experimental import pallas as pl
from jax.experimental.pallas import tpu as pltpu
from jax.sharding import PartitionSpec as P

MESH = pl.DeviceIdType.MESH
F32, BF16 = jnp.float32, jnp.bfloat16
HIGH = lax.Precision.HIGHEST

NX, NY, NZ, NC = 4, 4, 8, 2
NROW = NZ * NC
NCTX = NY * NROW
ROWS, CH, STATE, BLOCK, HEADS, HD = 512, 512, 128, 256, 8, 64
FEAT, HALF = 256, 128
Q, QW = 4, 128
ZFIRST = 3
TILE, NT = 128, 4
XT, XR = 2, 256


def dot(a, b, dims, precision=None):
    return lax.dot_general(a, b, (dims, ((), ())), precision=precision, preferred_element_type=F32)


def remote(src, dst, send, recv, ctx, ten):
    return pltpu.make_async_remote_copy(
        src_ref=src, dst_ref=dst, send_sem=send, recv_sem=recv,
        device_id=(ctx, ten), device_id_type=MESH,
    )


def kernel(
    lay_h, vp_h, taps_h, pre_h, sin_h, sout_h, step_h, ld_h, skip_h, go_h,
    gi_ref, gv_ref,
    lay, vp, taps, pre, sin, sout, step, ld, skip, go,
    cum, a_ref, b_ref, gc, gp, bs1, clos, lt,
    s_send, s_recv, later, z_send, z_recv, rsuf, lsuf, y_send, y_recv, c_send, c_recv, m_send, carry,
    xo_send, xo_recv, xd_send, xd_recv, x_keep, x_own,
    w_acc, w_send, w_recv, w_own, v_send, v_recv, u_own, u_send, u_recv, zf_send, zf_recv, zf_own, yf_send, yf_recv,
    in_sem, lay_ss, lay_rs, s_ss, s_rs, z_ss, z_rs, y_ss, y_rs, c_ss, c_rs, m_ss, m_rs, h_ss, h_rs,
    xo_ss, xo_rs, xd_ss, xd_rs, w_ss, w_rs, v_ss, v_rs, u_ss, u_rs, zf_ss, zf_rs, yf_ss, yf_rs,
):
    c = lax.axis_index("context")
    t = lax.axis_index("tensor")
    core = lax.rem(c, NC)
    other = 1 - core
    z = lax.rem(c // NC, NZ)
    y = c // NROW
    row0 = y * NROW + core
    nxt, prv = lax.rem(c + 1, NCTX), lax.rem(c + NCTX - 1, NCTX)
    mate = c + 1 - 2 * core
    xs = [lax.rem(t + k, NX) for k in range(NX)]
    ys = [lax.rem(y + k, NY) for k in range(NY)]
    yc = [lax.rem(c + k * NROW, NCTX) for k in range(NY)]
    zs = [lax.rem(z + k, NZ) for k in range(NZ)]
    zc = [row0 + k * NC for k in zs]

    def slab(k, n):
        return pl.ds(pl.multiple_of(k * n, n), n)

    loads = {}

    def load(name, src, dst):
        loads[name] = pltpu.make_async_copy(src, dst, in_sem.at[len(loads)])
        loads[name].start()

    load("ld", ld_h, ld)
    load("go", go_h, go)
    load("sout", sout_h, sout)

    barrier = pltpu.get_barrier_semaphore()
    partners = [(zc[k], t) for k in range(1, NZ)] + [(yc[k], t) for k in range(1, NY)]
    partners += [(c, xs[1]), (c, xs[3]), (nxt, t), (prv, t)]
    for ctx, ten in partners:
        pl.semaphore_signal(barrier, inc=1, device_id=(ctx, ten), device_id_type=MESH)

    load("sin", sin_h, sin)
    load("step", step_h, step)
    load("skip", skip_h, skip)
    load("pre", pre_h, pre)
    load("taps", taps_h, taps)
    load("vp", vp_h, vp)
    load("lay", lay_h, lay.at[t])

    def pieces(v):
        parts = []
        for _ in range(3):
            parts.append(v.astype(BF16))
            v = v - parts[-1].astype(F32)
        return parts

    ri = lax.broadcasted_iota(jnp.int32, (BLOCK, BLOCK), 0)
    ci = lax.broadcasted_iota(jnp.int32, (BLOCK, BLOCK), 1)
    upto = jnp.where(ri <= ci, 1.0, 0.0).astype(BF16)
    hi = lax.broadcasted_iota(jnp.int32, (HEADS, CH), 0)
    li = lax.broadcasted_iota(jnp.int32, (HEADS, CH), 1)
    onehot = (li // HD == hi).astype(F32)
    hi3 = lax.broadcasted_iota(jnp.int32, (3 * HEADS, CH), 0)
    li3 = lax.broadcasted_iota(jnp.int32, (3 * HEADS, CH), 1)
    onehot3 = jnp.where(li3 // HD == lax.rem(hi3, HEADS), 1.0, 0.0).astype(BF16)
    loads["ld"].wait()
    for k in range(2):
        cols = slice(k * BLOCK, (k + 1) * BLOCK)
        sums = [dot(p, upto, ((1,), (0,))) for p in pieces(ld[:, cols])]
        cum[:, cols] = (sums[2] + sums[1]) + sums[0]
    cum3 = jnp.concatenate([p.astype(F32) for p in pieces(cum[...])], axis=0).astype(BF16)
    for k in range(2):
        rows = slice(k * BLOCK, (k + 1) * BLOCK)
        b_ref[rows, :] = dot(cum3[:, rows], onehot3, ((0,), (0,)))
    clos0 = b_ref[BLOCK - 1:BLOCK, :]
    clos1 = b_ref[2 * BLOCK - 1:2 * BLOCK, :]
    clos[0:1, :] = clos0
    clos[1:2, :] = clos1
    for k in range(NC):
        s_send[k, STATE:STATE + 8, :] = jnp.broadcast_to((clos0 + clos1)[:, k * 256:(k + 1) * 256], (8, 256))

    loads["go"].wait()
    loads["sout"].wait()
    s_copy = remote(s_send.at[other], s_recv, s_ss, s_rs, mate, t)
    for half in (other, core):
        lanes = slab(half, 256)
        states = []
        for k in range(2):
            rows = slice(k * BLOCK, (k + 1) * BLOCK)
            w = (go[rows, lanes].astype(F32) * jnp.exp(b_ref[rows, lanes])).astype(BF16)
            states.append(dot(sout[rows, :], w, ((0,), (0,))))
        bs1[:, lanes] = states[1]
        s_send[half, 0:STATE, :] = states[0] + jnp.exp(clos[0:1, lanes]) * states[1]
        if half is other:
            pl.semaphore_wait(barrier, len(partners))
            s_copy.start()

    remote(lay_h, lay.at[t], lay_ss.at[0], lay_rs.at[0], c, xs[1]).start()
    remote(lay_h, lay.at[t], lay_ss.at[1], lay_rs.at[1], c, xs[3]).start()

    def within(k):
        rows = slice(k * BLOCK, (k + 1) * BLOCK)
        scores = dot(sin[rows, :], sout[rows, :], ((1,), (1,)))
        scores = jnp.where(ci >= ri, scores, 0.0)
        low = lax.broadcasted_iota(jnp.int32, (BLOCK, 128), 1) < HD
        cum_t = cum[:, rows].T
        for pair in range(HEADS // 2):
            lanes = slice(pair * 128, pair * 128 + 128)
            g = go[rows, lanes]
            parts = []
            for h in (2 * pair, 2 * pair + 1):
                spread = cum[h:h + 1, rows] - cum_t[:, h:h + 1]
                weights = (scores * jnp.exp(jnp.minimum(spread, 0.0))).astype(BF16)
                parts.append(dot(weights, g, ((1,), (0,))))
            a_ref[rows, lanes] = jnp.where(low, parts[0], parts[1])

    loads["sin"].wait()
    within(0)

    s_copy.wait_recv()
    first = jnp.where(core == 0, s_send[core], s_recv[...])
    second = jnp.where(core == 0, s_recv[...], s_send[core])
    later[...] = second
    d_first, d_second = first[STATE:STATE + 1, :], second[STATE:STATE + 1, :]
    chip = first[0:STATE, :] + jnp.exp(d_first) * second[0:STATE, :]
    z_send[:, 0:256] = chip.astype(BF16)
    d_chip = d_first + d_second
    row = lax.broadcasted_iota(jnp.int32, (16, 128), 0)

    def packed(d):
        out = jnp.zeros((16, 128), F32)
        for n, piece in enumerate(pieces(d)):
            piece = piece.astype(F32)
            out = jnp.where(row == 2 * n, piece[:, 0:128], out)
            out = jnp.where(row == 2 * n + 1, piece[:, 128:256], out)
        return out.astype(BF16)

    def unpacked(got):
        return jnp.concatenate([got[n:n + 1, :] + got[n + 2:n + 3, :] + got[n + 4:n + 5, :] for n in range(2)], axis=1)

    extra = packed(d_chip)
    for n in range(NZ):
        z_send[n * 16:(n + 1) * 16, 256:384] = extra
    for k in (4, 3, 5, 2, 6, 1, 7):
        remote(z_send.at[slab(zs[k], 16)], z_recv.at[z], z_ss, z_rs, zc[k], t).start()
    z_recv[z] = z_send[slab(z, 16), :]

    within(1)

    remote(z_send.at[pl.ds(0, 112)], z_recv.at[pl.ds(0, NZ - 1)], z_ss, z_rs, c, t).wait_recv()
    spans = [unpacked(z_recv[j][:, 256:384].astype(F32)) for j in range(NZ)]
    decays = [jnp.exp(d) for d in spans]
    r = jnp.zeros((16, 256), F32)
    for j in range(NZ - 1, -1, -1):
        rsuf[j] = r
        r = z_recv[j][:, 0:256].astype(F32) + decays[j] * r
    y_send[:, 0:256] = r.astype(BF16)
    y_send[:, 256:384] = packed(sum(spans[1:], spans[0]))
    for k in (2, 1, 3):
        remote(y_send, y_recv.at[y], y_ss, y_rs, yc[k], t).start()
    y_recv[y] = y_send[...]
    l = jnp.zeros((1, 256), F32)
    for j in range(NZ - 1, -1, -1):
        lsuf[j] = jnp.exp(l)
        l = l + spans[j]

    for k, n in ((3, 0), (1, 1)):
        remote(lay_h, lay.at[xs[k]], lay_ss.at[n], lay_rs.at[n], c, t).wait_recv()
        half = pl.ds(n * 256, 256)
        block = lay.at[xs[k], half]
        remote(block, block, lay_ss.at[2 + n], lay_rs.at[2 + n], c, xs[4 - k]).start()

    for name in ("step", "skip", "pre"):
        loads[name].wait()
    skip_e = dot(skip[...], onehot, ((1,), (0,)), HIGH)

    def factors(n):
        rows = slice(n * 64, (n + 1) * 64)
        close = clos[n // 4:n // 4 + 1, :]
        v = pre[rows, :].astype(F32)
        sig = 1.0 / (1.0 + jnp.exp(-v))
        slope = sig * (1.0 + v * (1.0 - sig))
        step_e = dot(step[:, rows], onehot, ((0,), (0,)), HIGH)
        a_ref[rows, :] = (step_e * a_ref[rows, :] + skip_e * go[rows, :].astype(F32)) * slope
        b_ref[rows, :] = step_e * jnp.exp(close - b_ref[rows, :]) * slope

    for n in range(4):
        factors(n)

    remote(y_send, y_recv.at[pl.ds(0, NY - 1)], y_ss, y_rs, c, t).wait_recv()
    coming = jnp.zeros((16, 256), F32)
    for yy in range(NY - 1, 0, -1):
        got = y_recv[yy].astype(F32)
        coming = jnp.where(yy > y, got[:, 0:256] + jnp.exp(unpacked(got[:, 256:384])) * coming, coming)
    for k in (4, 3, 5, 2, 6, 1, 7, 0):
        c_send[slab(zs[k], 16), :] = (rsuf[zs[k]] + lsuf[zs[k]] * coming).astype(BF16)
        if k:
            remote(c_send.at[slab(zs[k], 16)], c_recv.at[slab(z, 16)], c_ss, c_rs, zc[k], t).start()
    c_recv[slab(z, 16), :] = c_send[slab(z, 16), :]

    for n in range(4, 8):
        factors(n)

    def transposed(x):
        for half in range(2):
            cols = slice(half * 256, half * 256 + 256)
            tr = lay[x, cols, :].T
            for zz in range(NZ):
                for cc in range(NC):
                    f0 = (zz * NC + cc) * 16
                    lt[cc, pl.ds(pl.multiple_of(x * 128 + zz * 16, 16), 16), cols] = tr[f0:f0 + 16, :]

    loads["lay"].wait()
    for k in (0, 1, 3):
        transposed(xs[k])
    for n, rows in ((0, pl.ds(0, 256)), (1, pl.ds(256, 256))):
        block = lay.at[xs[2], rows]
        remote(block, block, lay_ss.at[2 + n], lay_rs.at[2 + n], c, t).wait_recv()
    transposed(xs[2])
    for name in ("taps", "vp"):
        loads[name].wait()
    decay_second = jnp.exp(later[STATE:STATE + 1, :])

    remote(c_send, c_recv.at[pl.ds(0, 112)], c_ss, c_rs, c, t).wait_recv()
    into_second = c_recv[...]
    into_first = (later[0:STATE, :] + decay_second * into_second.astype(F32)).astype(BF16)
    m_send[...] = jnp.where(core == 0, into_second, into_first)
    m_copy = remote(m_send, carry.at[core], m_ss, m_rs, mate, t)
    m_copy.start()
    carry[core] = jnp.where(core == 0, into_first, into_second)

    halo = remote(gc.at[pl.ds(0, 8)], gc.at[pl.ds(ROWS, 8)], h_ss, h_rs, prv, t)

    def conv_grad(rows, lanes, carried):
        value = a_ref[rows, lanes] + b_ref[rows, lanes] * dot(sin[rows, :], carried, ((1,), (0,)))
        gc[rows, lanes] = value.astype(BF16).astype(F32)

    for half in (core, other):
        lanes = slab(half, 256)
        if half is other:
            remote(m_send, carry.at[other], m_ss, m_rs, mate, t).wait_recv()
        into_last = carry[half]
        into_block = (bs1[:, lanes] + jnp.exp(clos[1:2, lanes]) * into_last.astype(F32)).astype(BF16)
        conv_grad(slice(0, 16), lanes, into_block)
        if half is other:
            halo.start()
        conv_grad(slice(16, TILE), lanes, into_block)
        for n in range(1, NT):
            conv_grad(slice(n * TILE, (n + 1) * TILE), lanes, into_block if n < NT // 2 else into_last)

    def weights_of(k):
        return vp[slab(xs[k], FEAT), :]

    def proj_grad(n):
        r0 = n * TILE
        summed = taps[0:1, :] * gc[r0 + 3:r0 + 3 + TILE, :]
        for j in range(1, 4):
            summed = summed + taps[j:j + 1, :] * gc[r0 + 3 - j:r0 + 3 - j + TILE, :]
        gp[r0:r0 + TILE, :] = summed.astype(BF16)

    def far_start(n):
        part = dot(gp[n * XR:(n + 1) * XR, :], weights_of(2), ((1,), (1,)))
        for s in range(2):
            xo_send[n, s] = part[:, s * HALF:(s + 1) * HALF].astype(BF16)
            remote(xo_send.at[n, s], xo_recv.at[n, s], xo_ss, xo_rs.at[n, s], c, xs[(1, 3)[s]]).start()

    proj_grad(0)
    proj_grad(1)
    far_start(0)
    proj_grad(2)
    early = (NT - 1) * TILE
    for h in range(2):
        lanes = slice(h * 256, (h + 1) * 256)
        w_acc[:, lanes] = dot(lt[other, :, 0:early], gp[0:early, lanes], ((1,), (0,)))
    halo.wait_recv()
    gc[ROWS:ROWS + 8, :] = jnp.where(c == NCTX - 1, 0.0, gc[ROWS:ROWS + 8, :])
    proj_grad(3)

    def w_copy(q):
        return remote(w_send.at[q], w_recv.at[q], w_ss.at[q], w_rs.at[q], mate, t)

    for h in range(2):
        lanes = slice(h * 256, (h + 1) * 256)
        part = w_acc[:, lanes] + dot(lt[other, :, early:ROWS], gp[early:ROWS, lanes], ((1,), (0,)))
        for q in (2 * h, 2 * h + 1):
            w_send[q] = part[:, (q % 2) * QW:(q % 2 + 1) * QW].astype(BF16)
            w_copy(q).start()
    far_start(1)

    def xd_start(n, s, half):
        remote(xd_send.at[n, s, half], xd_recv.at[n, s, half], xd_ss, xd_rs.at[n, s, half], c, xs[(1, 3)[s]]).start()

    def near_start(n):
        for s in range(2):
            part = dot(gp[n * XR:(n + 1) * XR, :], weights_of((1, 3)[s]), ((1,), (1,)))
            xd_send[n, s, 1 - s] = part[:, (1 - s) * HALF:(2 - s) * HALF].astype(BF16)
            xd_start(n, s, 1 - s)
            x_keep[n, s] = part[:, s * HALF:(s + 1) * HALF]

    near_start(0)
    for h in range(2):
        part = dot(lt[core], gp[:, h * 256:(h + 1) * 256], ((1,), (0,)))
        for q in (2 * h, 2 * h + 1):
            w_own[q] = part[:, (q % 2) * QW:(q % 2 + 1) * QW]

    for q in (0, ZFIRST, 1, 2):
        w_copy(q).wait_recv()
        w_own[q] = w_own[q] + w_recv[q].astype(F32)
        if q == ZFIRST:
            for zz in range(NZ):
                for yy in range(NY):
                    r0 = yy * 128 + zz * 16
                    zf_send[zz, yy * 16:(yy + 1) * 16, :] = w_own[q, r0:r0 + 16, :].astype(BF16)
            for k in (4, 3, 5, 2, 6, 1, 7):
                remote(zf_send.at[zs[k]], zf_recv.at[z], zf_ss, zf_rs, zc[k], t).start()
        else:
            for k in (2, 1, 3):
                v_send[q, ys[k]] = w_own[q, slab(ys[k], 128), :].astype(BF16)
                remote(v_send.at[q, ys[k]], v_recv.at[q, y], v_ss.at[q], v_rs.at[q], yc[k], t).start()
    near_start(1)
    x_own[...] = dot(gp[...], weights_of(0), ((1,), (1,)))

    for n in range(XT):
        for s in range(2):
            remote(xo_send.at[n, s], xo_recv.at[n, s], xo_ss, xo_rs.at[n, s], c, t).wait_recv()
            xd_send[n, s, s] = (x_keep[n, s] + xo_recv[n, s].astype(F32)).astype(BF16)
            xd_start(n, s, s)

    def to_z(q):
        remote(v_send.at[q, pl.ds(0, NY - 1)], v_recv.at[q, pl.ds(0, NY - 1)], v_ss.at[q], v_rs.at[q], c, t).wait_recv()
        acc = w_own[q, slab(y, 128), :]
        for k in range(1, NY):
            acc = acc + v_recv[q, ys[k]].astype(F32)
        u_own[q] = acc
        u_send[q] = acc.astype(BF16)
        for k in (4, 3, 5, 2, 6, 1, 7):
            remote(u_send.at[q, slab(zs[k], 16)], u_recv.at[q, z], u_ss.at[q], u_rs.at[q], zc[k], t).start()

    def to_y():
        remote(zf_send.at[pl.ds(0, NZ - 1)], zf_recv.at[pl.ds(0, NZ - 1)], zf_ss, zf_rs, c, t).wait_recv()
        acc = jnp.concatenate([w_own[ZFIRST, pl.ds(pl.multiple_of(yy * 128 + z * 16, 16), 16), :] for yy in range(NY)], axis=0)
        for k in range(1, NZ):
            acc = acc + zf_recv[zs[k]].astype(F32)
        zf_own[...] = acc
        yf_send[...] = acc.astype(BF16)
        for k in (2, 1, 3):
            remote(yf_send.at[slab(ys[k], 16)], yf_recv.at[y], yf_ss, yf_rs, yc[k], t).start()

    to_z(0)
    to_z(1)
    to_y()
    to_z(2)

    for n in range(XT):
        rows = slice(n * XR, (n + 1) * XR)
        for half in range(2):
            lanes = slice(half * HALF, (half + 1) * HALF)
            acc = x_own[rows, lanes]
            for s in range(2):
                remote(xd_send.at[n, s, half], xd_recv.at[n, s, half], xd_ss, xd_rs.at[n, s, half], c, t).wait_recv()
                acc = acc + xd_recv[n, s, half].astype(F32)
            gi_ref[rows, lanes] = acc.astype(BF16)

    scale = 1.0 / math.sqrt(ROWS * NCTX)
    for q in (0, 1, ZFIRST, 2):
        if q == ZFIRST:
            remote(yf_send.at[pl.ds(0, 48)], yf_recv.at[pl.ds(0, NY - 1)], yf_ss, yf_rs, c, t).wait_recv()
            acc = zf_own[slab(y, 16), :]
            for k in range(1, NY):
                acc = acc + yf_recv[ys[k]].astype(F32)
        else:
            remote(u_send.at[q, pl.ds(0, 112)], u_recv.at[q, pl.ds(0, NZ - 1)], u_ss.at[q], u_rs.at[q], c, t).wait_recv()
            acc = u_own[q, slab(z, 16), :]
            for k in range(1, NZ):
                acc = acc + u_recv[q, zs[k]].astype(F32)
        gv_ref[:, q * QW:(q + 1) * QW] = acc * scale

    def sent(src, sem):
        remote(src, src, sem, h_rs, c, t).wait_send()

    sent(s_send.at[other], s_ss)
    sent(lay_h, lay_ss.at[0])
    sent(lay_h, lay_ss.at[1])
    sent(lay.at[0, pl.ds(0, 256)], lay_ss.at[2])
    sent(lay.at[0, pl.ds(0, 256)], lay_ss.at[3])
    sent(z_send.at[pl.ds(0, 112)], z_ss)
    sent(y_recv.at[pl.ds(0, NY - 1)], y_ss)
    sent(c_send.at[pl.ds(0, 112)], c_ss)
    sent(m_send, m_ss)
    sent(gc.at[pl.ds(0, 8)], h_ss)
    sent(xo_send, xo_ss)
    sent(xd_send, xd_ss)
    for q in range(Q):
        w_copy(q).wait_send()
        if q != ZFIRST:
            sent(v_send.at[q, pl.ds(0, NY - 1)], v_ss.at[q])
            sent(u_send.at[q, pl.ds(0, 112)], u_ss.at[q])
    sent(zf_send.at[pl.ds(0, NZ - 1)], zf_ss)
    sent(yf_send.at[pl.ds(0, 48)], yf_ss)


def local(layer_input, value_proj, conv_taps, conv_pre, state_in, state_out, step_size, log_decay, skip_gain, grad_out):
    dma = pltpu.SemaphoreType.DMA
    V = pltpu.VMEM
    scratch = [
        V((NX, ROWS, FEAT), BF16), V((NX * FEAT, CH), BF16), V((4, CH), F32), V((ROWS, CH), BF16),
        V((ROWS, STATE), BF16), V((ROWS, STATE), BF16), V((HEADS, ROWS), F32), V((HEADS, ROWS), F32),
        V((1, HEADS), F32), V((ROWS, CH), BF16),
        V((HEADS, ROWS), F32), V((ROWS, CH), F32), V((ROWS, CH), F32), V((ROWS + 8, CH), F32), V((ROWS, CH), BF16),
        V((STATE, CH), F32), V((8, CH), F32), V((NC, ROWS, ROWS), BF16),
        V((NC, STATE + 8, 256), F32), V((STATE + 8, 256), F32), V((STATE + 8, 256), F32),
        V((STATE, 384), BF16), V((NZ, 16, 384), BF16), V((NZ, 16, 256), F32), V((NZ, 1, 256), F32),
        V((16, 384), BF16), V((NY, 16, 384), BF16),
        V((STATE, 256), BF16), V((STATE, 256), BF16), V((STATE, 256), BF16), V((NC, STATE, 256), BF16),
        V((XT, 2, XR, HALF), BF16), V((XT, 2, XR, HALF), BF16), V((XT, 2, 2, XR, HALF), BF16), V((XT, 2, 2, XR, HALF), BF16),
        V((XT, 2, XR, HALF), F32), V((ROWS, FEAT), F32),
        V((512, CH), F32), V((Q, 512, QW), BF16), V((Q, 512, QW), BF16), V((Q, 512, QW), F32),
        V((Q, NY, 128, QW), BF16), V((Q, NY, 128, QW), BF16), V((Q, 128, QW), F32), V((Q, 128, QW), BF16), V((Q, NZ, 16, QW), BF16),
        V((NZ, 64, QW), BF16), V((NZ, 64, QW), BF16), V((64, QW), F32), V((64, QW), BF16), V((NY, 16, QW), BF16),
        dma((10,)), dma((4,)), dma((4,)), dma, dma, dma, dma, dma, dma, dma, dma, dma, dma, dma, dma,
        dma, dma((XT, 2)), dma, dma((XT, 2, 2)), dma((Q,)), dma((Q,)), dma((Q,)), dma((Q,)), dma((Q,)), dma((Q,)), dma, dma, dma, dma,
    ]
    outs = (V((ROWS, FEAT), BF16), V((16, CH), F32))
    return pl.pallas_call(
        kernel,
        out_shape=outs,
        in_specs=[pl.BlockSpec(memory_space=pl.ANY)] * 10,
        out_specs=(pl.BlockSpec(memory_space=pltpu.VMEM), pl.BlockSpec(memory_space=pltpu.VMEM)),
        scratch_shapes=scratch,
        compiler_params=pltpu.CompilerParams(
            collective_id=0, has_side_effects=True, vmem_limit_bytes=60 * 2**20
        ),
        cost_estimate=pl.CostEstimate(flops=1_500_000_000, bytes_accessed=4_000_000, transcendentals=2_000_000),
        name="scan_backward",
    )(
        layer_input, value_proj, conv_taps, conv_pre, state_in, state_out, step_size, log_decay,
        skip_gain.reshape(1, HEADS), grad_out,
    )


def solution(mesh):
    return jax.shard_map(
        local,
        mesh=mesh,
        in_specs=(
            P("context", "tensor"),
            P(None, "tensor"),
            P(None, "tensor"),
            P("context", "tensor"),
            P("context", None),
            P("context", None),
            P("tensor", "context"),
            P("tensor", "context"),
            P("tensor"),
            P("context", "tensor"),
        ),
        out_specs=(P("context", "tensor"), P("context", "tensor")),
        check_vma=False,
    )
```

time: 54.5 us -> 42.8 us (0.79)
  Pallas kernels: 53.8 us -> 40.7 us
  local copies, waits for them, and re-layouts: 0 us -> 1.32 us
    pallas_call x1 -> x0, Pallas kernels: 10.1 us -> none  [local(): pl.pallas_call(place, out_shape=outs, in_specs=[pl.BlockSpec(memory_space...]
    pallas_call x1, Pallas kernels: 43.7 us -> 40.7 us  [local(): pl.pallas_call(kernel, out_shape=outs, in_specs=[pl.BlockSpec(memory_spac...]
    unnamed x0 -> x2, local copies, waits for them, and re-layouts: none -> 1.32 us
where the time goes in v3:
time: 42.8 us; the launch traced here: 42.7 us
  Pallas kernels  40.7 us (95%)
  local copies, waits for them, and re-layouts  1.32 us (3%)
  between operations  0.64 us (1%)
    pallas_call x1, Pallas kernels, local(): pl.pallas_call(kernel, out_shape=outs, in_specs=[pl.BlockSpec(memory_spac...  40.7 us
    unnamed x2, local copies, waits for them, and re-layouts  1.32 us

profile of v3, /device:TPU:1, one launch (start us, length us, event | category | flops | bytes accessed | tf_op | source)
XLA Modules:
  0.0 42.7 jit_solution(4083837447274772271)
XLA Ops:
  0.6 40.7 %scan_backward.1 = (bf16[512,256]{1,0:T(8,128)(2,1)S(1)}, f32[16,512]{1,0:T(8,128)S(1)}) custom-call(bf16[512,256]{1,0:T(8,128)(2,1)} %lay_h.1, bf16[1024,512]{1,0:T(8,128)(2,1)} %vp_h.1, f32[4,512]{1,0:T(4,128)} %taps_h.1, bf16[512,512]{1,0:T(8,128)(2,1)} %pre_h.1, bf16[512,128]{1,0:T(8,128)(2,1)} %sin_h.1, bf16[512,128]{1,0:T(8,128)(2,1)} %sout_h.1, ...), custom_call_target="tpu_custom_call" | custom-call | flops 1500000000 | bytes 4000000 | tf_op jit(solution)/shard_map/scan_backward/pallas_call | solution.py:464
  41.3 0.7 %copy.14 = bf16[512,256]{1,0:T(8,128)(2,1)} copy(bf16[512,256]{1,0:T(8,128)(2,1)S(1)} %get-tuple-element.2) | data formatting | bytes 524288
  42.0 0.6 %copy.15 = f32[16,512]{1,0:T(8,128)} copy(f32[16,512]{1,0:T(8,128)S(1)} %get-tuple-element.3) | data formatting | bytes 65536

commit v4 on v3

--- a/solution.py
+++ b/solution.py
@@ -20,7 +20,7 @@
 Q, QW = 4, 128
 ZFIRST = 3
 TILE, NT = 128, 4
-XT, XR = 2, 256
+PIECES = ((0, 256), (256, 240), (496, 16))
 
 
 def dot(a, b, dims, precision=None):
@@ -40,10 +40,10 @@
     lay, vp, taps, pre, sin, sout, step, ld, skip, go,
     cum, a_ref, b_ref, gc, gp, bs1, clos, lt,
     s_send, s_recv, later, z_send, z_recv, rsuf, lsuf, y_send, y_recv, c_send, c_recv, m_send, carry,
-    xo_send, xo_recv, xd_send, xd_recv, x_keep, x_own,
-    w_acc, w_send, w_recv, w_own, v_send, v_recv, u_own, u_send, u_recv, zf_send, zf_recv, zf_own, yf_send, yf_recv,
+    xo_send, xo_recv, xd_send, xd_recv, xf_send, xf_recv, x_keep, x_own,
+    layh, lth, ltm, lthm, gpm, gpe, hb, w_own, v_send, v_recv, u_own, u_send, u_recv, zf_send, zf_recv, zf_own, yf_send, yf_recv,
     in_sem, lay_ss, lay_rs, s_ss, s_rs, z_ss, z_rs, y_ss, y_rs, c_ss, c_rs, m_ss, m_rs, h_ss, h_rs,
-    xo_ss, xo_rs, xd_ss, xd_rs, w_ss, w_rs, v_ss, v_rs, u_ss, u_rs, zf_ss, zf_rs, yf_ss, yf_rs,
+    xo_ss, xo_rs, xd_ss, xd_rs, lt_ss, lt_rs, g_ss, g_rs, v_ss, v_rs, u_ss, u_rs, zf_ss, zf_rs, yf_ss, yf_rs, lh_ss, lh_rs, xf_ss, xf_rs,
 ):
     c = lax.axis_index("context")
     t = lax.axis_index("tensor")
@@ -75,7 +75,7 @@
 
     barrier = pltpu.get_barrier_semaphore()
     partners = [(zc[k], t) for k in range(1, NZ)] + [(yc[k], t) for k in range(1, NY)]
-    partners += [(c, xs[1]), (c, xs[3]), (nxt, t), (prv, t)]
+    partners += [(c, xs[1]), (c, xs[2]), (c, xs[3]), (nxt, t), (prv, t)]
     for ctx, ten in partners:
         pl.semaphore_signal(barrier, inc=1, device_id=(ctx, ten), device_id_type=MESH)
 
@@ -257,6 +257,13 @@
         block = lay.at[xs[2], rows]
         remote(block, block, lay_ss.at[2 + n], lay_rs.at[2 + n], c, t).wait_recv()
     transposed(xs[2])
+    lh_copy = remote(lay.at[pl.ds(0, NX), pl.ds(ROWS - 16, 16)], layh, lh_ss, lh_rs, nxt, t)
+    lh_copy.start()
+    lt_copy = remote(lt.at[other], ltm, lt_ss.at[0], lt_rs.at[0], mate, t)
+    lt_copy.start()
+    gp[ROWS:ROWS + 128, :] = jnp.zeros((128, CH), BF16)
+    gpm[ROWS + 16:ROWS + 128, :] = jnp.zeros((112, CH), BF16)
+    gc[ROWS:ROWS + 8, :] = jnp.zeros((8, CH), F32)
     for name in ("taps", "vp"):
         loads[name].wait()
     decay_second = jnp.exp(later[STATE:STATE + 1, :])
@@ -269,7 +276,7 @@
     m_copy.start()
     carry[core] = jnp.where(core == 0, into_first, into_second)
 
-    halo = remote(gc.at[pl.ds(0, 8)], gc.at[pl.ds(ROWS, 8)], h_ss, h_rs, prv, t)
+    halo = remote(gc.at[pl.ds(0, 8)], hb, h_ss, h_rs, prv, t)
 
     def conv_grad(rows, lanes, carried):
         value = a_ref[rows, lanes] + b_ref[rows, lanes] * dot(sin[rows, :], carried, ((1,), (0,)))
@@ -278,6 +285,15 @@
     for half in (core, other):
         lanes = slab(half, 256)
         if half is other:
+            lh_copy.wait_recv()
+            for x in range(NX):
+                tr = jnp.concatenate([layh[x], jnp.zeros((112, FEAT), BF16)], axis=0).T
+                for zz in range(NZ):
+                    for cc in range(NC):
+                        f0 = (zz * NC + cc) * 16
+                        lth[cc, x * 128 + zz * 16:x * 128 + zz * 16 + 16, :] = tr[f0:f0 + 16, :]
+            lth_copy = remote(lth.at[other], lthm, lt_ss.at[1], lt_rs.at[1], mate, t)
+            lth_copy.start()
             remote(m_send, carry.at[other], m_ss, m_rs, mate, t).wait_recv()
         into_last = carry[half]
         into_block = (bs1[:, lanes] + jnp.exp(clos[1:2, lanes]) * into_last.astype(F32)).astype(BF16)
@@ -285,86 +301,122 @@
         if half is other:
             halo.start()
         conv_grad(slice(16, TILE), lanes, into_block)
-        for n in range(1, NT):
+        for n in range(1, NT if half is core else NT - 1):
             conv_grad(slice(n * TILE, (n + 1) * TILE), lanes, into_block if n < NT // 2 else into_last)
 
     def weights_of(k):
         return vp[slab(xs[k], FEAT), :]
 
-    def proj_grad(n):
-        r0 = n * TILE
-        summed = taps[0:1, :] * gc[r0 + 3:r0 + 3 + TILE, :]
+    def proj_grad(r0, count):
+        summed = taps[0:1, :] * gc[r0 + 3:r0 + 3 + count, :]
         for j in range(1, 4):
-            summed = summed + taps[j:j + 1, :] * gc[r0 + 3 - j:r0 + 3 - j + TILE, :]
-        gp[r0:r0 + TILE, :] = summed.astype(BF16)
+            summed = summed + taps[j:j + 1, :] * gc[r0 + 3 - j:r0 + 3 - j + count, :]
+        return summed.astype(BF16)
+
+    def g_copy(n):
+        rows = (pl.ds(0, 256), pl.ds(256, 272))[n]
+        return remote(gp.at[rows], gpm.at[rows], g_ss.at[n], g_rs.at[n], mate, t)
+
+    def piece_of(n, k):
+        r0, count = PIECES[n]
+        grad = gpe[...] if n == 2 else gp[r0:r0 + count, :]
+        return dot(grad, weights_of(k), ((1,), (1,)))
+
+    def xo_copy(n, s):
+        rows = pl.ds(*PIECES[n])
+        return remote(xo_send.at[s, rows], xo_recv.at[s, rows], xo_ss, xo_rs.at[n, s], c, xs[(1, 3)[s]])
+
+    def xd_copy(n, s, half):
+        rows = pl.ds(*PIECES[n])
+        return remote(xd_send.at[s, half, rows], xd_recv.at[s, half, rows], xd_ss, xd_rs.at[n, s, half], c, xs[(1, 3)[s]])
 
     def far_start(n):
-        part = dot(gp[n * XR:(n + 1) * XR, :], weights_of(2), ((1,), (1,)))
+        rows = slice(PIECES[n][0], sum(PIECES[n]))
+        part = piece_of(n, 2)
         for s in range(2):
-            xo_send[n, s] = part[:, s * HALF:(s + 1) * HALF].astype(BF16)
-            remote(xo_send.at[n, s], xo_recv.at[n, s], xo_ss, xo_rs.at[n, s], c, xs[(1, 3)[s]]).start()
-
-    proj_grad(0)
-    proj_grad(1)
-    far_start(0)
-    proj_grad(2)
-    early = (NT - 1) * TILE
+            xo_send[s, rows, :] = part[:, s * HALF:(s + 1) * HALF].astype(BF16)
+            xo_copy(n, s).start()
+
+    def near_start(n):
+        rows = slice(PIECES[n][0], sum(PIECES[n]))
+        for s in range(2):
+            part = piece_of(n, (1, 3)[s])
+            xd_send[s, 1 - s, rows, :] = part[:, (1 - s) * HALF:(2 - s) * HALF].astype(BF16)
+            xd_copy(n, s, 1 - s).start()
+            x_keep[s, rows, :] = part[:, s * HALF:(s + 1) * HALF]
+
+    def relay(n):
+        rows = slice(PIECES[n][0], sum(PIECES[n]))
+        for s in range(2):
+            xo_copy(n, s).wait_recv()
+            xd_send[s, s, rows, :] = (x_keep[s, rows, :] + xo_recv[s, rows, :].astype(F32)).astype(BF16)
+            xd_copy(n, s, s).start()
+
+    for n in range(NT):
+        gp[n * TILE:(n + 1) * TILE, :] = proj_grad(n * TILE, TILE)
+        if n == 1:
+            g_copy(0).start()
+            far_start(0)
+            conv_grad(slice((NT - 1) * TILE, ROWS), slab(other, 256), into_last)
+
+    row = lax.broadcasted_iota(jnp.int32, (16, CH), 0)
+    taps_now = [taps[j:j + 1, :] for j in range(3)]
+    head = [gc[j:j + 1, :] for j in range(3)]
+    ahead = jnp.zeros((16, CH), F32)
+    for n in range(3):
+        ahead = jnp.where(row == 13 + n, sum(taps_now[j] * head[n - j] for j in range(n + 1)), ahead)
+    gp[ROWS:ROWS + 16, :] = jnp.where(c == 0, 0.0, ahead).astype(BF16)
+    g_copy(1).start()
+
     for h in range(2):
         lanes = slice(h * 256, (h + 1) * 256)
-        w_acc[:, lanes] = dot(lt[other, :, 0:early], gp[0:early, lanes], ((1,), (0,)))
-    halo.wait_recv()
-    gc[ROWS:ROWS + 8, :] = jnp.where(c == NCTX - 1, 0.0, gc[ROWS:ROWS + 8, :])
-    proj_grad(3)
-
-    def w_copy(q):
-        return remote(w_send.at[q], w_recv.at[q], w_ss.at[q], w_rs.at[q], mate, t)
-
+        part = dot(lt[core], gp[0:ROWS, lanes], ((1,), (0,))) + dot(lth[core], gp[ROWS:ROWS + 128, lanes], ((1,), (0,)))
+        for q in (2 * h, 2 * h + 1):
+            w_own[q] = part[:, (q % 2) * QW:(q % 2 + 1) * QW]
+
+    far_start(1)
+
+    lt_copy.wait_recv()
+    lth_copy.wait_recv()
+    for n in range(2):
+        g_copy(n).wait_recv()
     for h in range(2):
         lanes = slice(h * 256, (h + 1) * 256)
-        part = w_acc[:, lanes] + dot(lt[other, :, early:ROWS], gp[early:ROWS, lanes], ((1,), (0,)))
+        part = dot(ltm[...], gpm[0:ROWS, lanes], ((1,), (0,))) + dot(lthm[...], gpm[ROWS:ROWS + 128, lanes], ((1,), (0,)))
         for q in (2 * h, 2 * h + 1):
-            w_send[q] = part[:, (q % 2) * QW:(q % 2 + 1) * QW].astype(BF16)
-            w_copy(q).start()
-    far_start(1)
-
-    def xd_start(n, s, half):
-        remote(xd_send.at[n, s, half], xd_recv.at[n, s, half], xd_ss, xd_rs.at[n, s, half], c, xs[(1, 3)[s]]).start()
-
-    def near_start(n):
-        for s in range(2):
-            part = dot(gp[n * XR:(n + 1) * XR, :], weights_of((1, 3)[s]), ((1,), (1,)))
-            xd_send[n, s, 1 - s] = part[:, (1 - s) * HALF:(2 - s) * HALF].astype(BF16)
-            xd_start(n, s, 1 - s)
-            x_keep[n, s] = part[:, s * HALF:(s + 1) * HALF]
+            total = w_own[q] + part[:, (q % 2) * QW:(q % 2 + 1) * QW]
+            w_own[q] = total
+            total = total.astype(BF16)
+            if q == ZFIRST:
+                for zz in range(NZ):
+                    for yy in range(NY):
+                        r0 = yy * 128 + zz * 16
+                        zf_send[zz, yy * 16:(yy + 1) * 16, :] = total[r0:r0 + 16, :]
+                for k in (4, 3, 5, 2, 6, 1, 7):
+                    remote(zf_send.at[zs[k]], zf_recv.at[z], zf_ss, zf_rs, zc[k], t).start()
+            else:
+                for yy in range(NY):
+                    v_send[q, yy] = total[yy * 128:(yy + 1) * 128, :]
+                for k in (2, 1, 3):
+                    remote(v_send.at[q, ys[k]], v_recv.at[q, y], v_ss.at[q], v_rs.at[q], yc[k], t).start()
 
     near_start(0)
-    for h in range(2):
-        part = dot(lt[core], gp[:, h * 256:(h + 1) * 256], ((1,), (0,)))
-        for q in (2 * h, 2 * h + 1):
-            w_own[q] = part[:, (q % 2) * QW:(q % 2 + 1) * QW]
-
-    for q in (0, ZFIRST, 1, 2):
-        w_copy(q).wait_recv()
-        w_own[q] = w_own[q] + w_recv[q].astype(F32)
-        if q == ZFIRST:
-            for zz in range(NZ):
-                for yy in range(NY):
-                    r0 = yy * 128 + zz * 16
-                    zf_send[zz, yy * 16:(yy + 1) * 16, :] = w_own[q, r0:r0 + 16, :].astype(BF16)
-            for k in (4, 3, 5, 2, 6, 1, 7):
-                remote(zf_send.at[zs[k]], zf_recv.at[z], zf_ss, zf_rs, zc[k], t).start()
-        else:
-            for k in (2, 1, 3):
-                v_send[q, ys[k]] = w_own[q, slab(ys[k], 128), :].astype(BF16)
-                remote(v_send.at[q, ys[k]], v_recv.at[q, y], v_ss.at[q], v_rs.at[q], yc[k], t).start()
     near_start(1)
-    x_own[...] = dot(gp[...], weights_of(0), ((1,), (1,)))
-
-    for n in range(XT):
-        for s in range(2):
-            remote(xo_send.at[n, s], xo_recv.at[n, s], xo_ss, xo_rs.at[n, s], c, t).wait_recv()
-            xd_send[n, s, s] = (x_keep[n, s] + xo_recv[n, s].astype(F32)).astype(BF16)
-            xd_start(n, s, s)
+
+    halo.wait_recv()
+    gc[ROWS:ROWS + 8, :] = jnp.where(c == NCTX - 1, 0.0, hb[...])
+    gpe[...] = proj_grad(ROWS - 16, 16)
+    xf_send[...] = piece_of(2, 2).astype(BF16)
+    xf_copy = remote(xf_send, xf_recv, xf_ss, xf_rs, c, xs[2])
+    xf_copy.start()
+    last = slice(PIECES[2][0], ROWS)
+    for s in range(2):
+        part = piece_of(2, (1, 3)[s]).astype(BF16)
+        for half in range(2):
+            xd_send[s, half, last, :] = part[:, half * HALF:(half + 1) * HALF]
+            xd_copy(2, s, half).start()
+    for n in range(3):
+        x_own[PIECES[n][0]:sum(PIECES[n]), :] = piece_of(n, 0)
 
     def to_z(q):
         remote(v_send.at[q, pl.ds(0, NY - 1)], v_recv.at[q, pl.ds(0, NY - 1)], v_ss.at[q], v_rs.at[q], c, t).wait_recv()
@@ -386,19 +438,25 @@
         for k in (2, 1, 3):
             remote(yf_send.at[slab(ys[k], 16)], yf_recv.at[y], yf_ss, yf_rs, yc[k], t).start()
 
+    relay(0)
+    relay(1)
     to_z(0)
     to_z(1)
     to_y()
     to_z(2)
 
-    for n in range(XT):
-        rows = slice(n * XR, (n + 1) * XR)
+    for n in range(3):
+        rows = slice(PIECES[n][0], sum(PIECES[n]))
         for half in range(2):
             lanes = slice(half * HALF, (half + 1) * HALF)
             acc = x_own[rows, lanes]
+            if n == 2:
+                if half == 0:
+                    xf_copy.wait_recv()
+                acc = acc + xf_recv[:, lanes].astype(F32)
             for s in range(2):
-                remote(xd_send.at[n, s, half], xd_recv.at[n, s, half], xd_ss, xd_rs.at[n, s, half], c, t).wait_recv()
-                acc = acc + xd_recv[n, s, half].astype(F32)
+                xd_copy(n, s, half).wait_recv()
+                acc = acc + xd_recv[s, half, rows, :].astype(F32)
             gi_ref[rows, lanes] = acc.astype(BF16)
 
     scale = 1.0 / math.sqrt(ROWS * NCTX)
@@ -428,13 +486,18 @@
     sent(c_send.at[pl.ds(0, 112)], c_ss)
     sent(m_send, m_ss)
     sent(gc.at[pl.ds(0, 8)], h_ss)
-    sent(xo_send, xo_ss)
+    sent(xo_send.at[pl.ds(0, 2), pl.ds(0, PIECES[2][0])], xo_ss)
+    xf_copy.wait_send()
     sent(xd_send, xd_ss)
     for q in range(Q):
-        w_copy(q).wait_send()
         if q != ZFIRST:
             sent(v_send.at[q, pl.ds(0, NY - 1)], v_ss.at[q])
             sent(u_send.at[q, pl.ds(0, 112)], u_ss.at[q])
+    sent(layh, lh_ss)
+    lt_copy.wait_send()
+    lth_copy.wait_send()
+    for n in range(2):
+        g_copy(n).wait_send()
     sent(zf_send.at[pl.ds(0, NZ - 1)], zf_ss)
     sent(yf_send.at[pl.ds(0, 48)], yf_ss)
 
@@ -446,19 +509,21 @@
         V((NX, ROWS, FEAT), BF16), V((NX * FEAT, CH), BF16), V((4, CH), F32), V((ROWS, CH), BF16),
         V((ROWS, STATE), BF16), V((ROWS, STATE), BF16), V((HEADS, ROWS), F32), V((HEADS, ROWS), F32),
         V((1, HEADS), F32), V((ROWS, CH), BF16),
-        V((HEADS, ROWS), F32), V((ROWS, CH), F32), V((ROWS, CH), F32), V((ROWS + 8, CH), F32), V((ROWS, CH), BF16),
+        V((HEADS, ROWS), F32), V((ROWS, CH), F32), V((ROWS, CH), F32), V((ROWS + 8, CH), F32), V((ROWS + 128, CH), BF16),
         V((STATE, CH), F32), V((8, CH), F32), V((NC, ROWS, ROWS), BF16),
         V((NC, STATE + 8, 256), F32), V((STATE + 8, 256), F32), V((STATE + 8, 256), F32),
         V((STATE, 384), BF16), V((NZ, 16, 384), BF16), V((NZ, 16, 256), F32), V((NZ, 1, 256), F32),
         V((16, 384), BF16), V((NY, 16, 384), BF16),
         V((STATE, 256), BF16), V((STATE, 256), BF16), V((STATE, 256), BF16), V((NC, STATE, 256), BF16),
-        V((XT, 2, XR, HALF), BF16), V((XT, 2, XR, HALF), BF16), V((XT, 2, 2, XR, HALF), BF16), V((XT, 2, 2, XR, HALF), BF16),
-        V((XT, 2, XR, HALF), F32), V((ROWS, FEAT), F32),
-        V((512, CH), F32), V((Q, 512, QW), BF16), V((Q, 512, QW), BF16), V((Q, 512, QW), F32),
+        V((2, ROWS, HALF), BF16), V((2, ROWS, HALF), BF16), V((2, 2, ROWS, HALF), BF16), V((2, 2, ROWS, HALF), BF16),
+        V((16, FEAT), BF16), V((16, FEAT), BF16), V((2, ROWS, HALF), F32), V((ROWS, FEAT), F32),
+        V((NX, 16, FEAT), BF16), V((NC, 512, 128), BF16), V((512, ROWS), BF16), V((512, 128), BF16), V((ROWS + 128, CH), BF16),
+        V((16, CH), BF16), V((8, CH), F32), V((Q, 512, QW), F32),
         V((Q, NY, 128, QW), BF16), V((Q, NY, 128, QW), BF16), V((Q, 128, QW), F32), V((Q, 128, QW), BF16), V((Q, NZ, 16, QW), BF16),
         V((NZ, 64, QW), BF16), V((NZ, 64, QW), BF16), V((64, QW), F32), V((64, QW), BF16), V((NY, 16, QW), BF16),
         dma((10,)), dma((4,)), dma((4,)), dma, dma, dma, dma, dma, dma, dma, dma, dma, dma, dma, dma,
-        dma, dma((XT, 2)), dma, dma((XT, 2, 2)), dma((Q,)), dma((Q,)), dma((Q,)), dma((Q,)), dma((Q,)), dma((Q,)), dma, dma, dma, dma,
+        dma, dma((3, 2)), dma, dma((3, 2, 2)), dma((2,)), dma((2,)), dma((2,)), dma((2,)), dma((Q,)), dma((Q,)), dma((Q,)), dma((Q,)), dma, dma, dma, dma, dma, dma,
+        dma, dma,
     ]
     outs = (V((ROWS, FEAT), BF16), V((16, CH), F32))
     return pl.pallas_call(

time: 42.8 us -> 41.2 us (0.963)
  Pallas kernels: 40.7 us -> 39.1 us
    pallas_call x1, Pallas kernels: 40.7 us -> 39.1 us  [local(): pl.pallas_call(kernel, out_shape=outs, in_specs=[pl.BlockSpec(memory_spac...]
where the time goes in v4:
time: 41.2 us; the launch traced here: 41 us
  Pallas kernels  39.1 us (95%)
  local copies, waits for them, and re-layouts  1.32 us (3%)
  between operations  0.64 us (2%)
    pallas_call x1, Pallas kernels, local(): pl.pallas_call(kernel, out_shape=outs, in_specs=[pl.BlockSpec(memory_spac...  39.1 us
    unnamed x2, local copies, waits for them, and re-layouts  1.32 us

profile of v4, /device:TPU:1, one launch (start us, length us, event | category | flops | bytes accessed | tf_op | source)
XLA Modules:
  0.0 41.0 jit_solution(4843529387882889428)
XLA Ops:
  0.6 39.1 %scan_backward.1 = (bf16[512,256]{1,0:T(8,128)(2,1)S(1)}, f32[16,512]{1,0:T(8,128)S(1)}) custom-call(bf16[512,256]{1,0:T(8,128)(2,1)} %lay_h.1, bf16[1024,512]{1,0:T(8,128)(2,1)} %vp_h.1, f32[4,512]{1,0:T(4,128)} %taps_h.1, bf16[512,512]{1,0:T(8,128)(2,1)} %pre_h.1, bf16[512,128]{1,0:T(8,128)(2,1)} %sin_h.1, bf16[512,128]{1,0:T(8,128)(2,1)} %sout_h.1, ...), custom_call_target="tpu_custom_call" | custom-call | flops 1500000000 | bytes 4000000 | tf_op jit(solution)/shard_map/scan_backward/pallas_call | solution.py:529
  39.7 0.7 %copy.14 = bf16[512,256]{1,0:T(8,128)(2,1)} copy(bf16[512,256]{1,0:T(8,128)(2,1)S(1)} %get-tuple-element.2) | data formatting | bytes 524288
  40.4 0.6 %copy.15 = f32[16,512]{1,0:T(8,128)} copy(f32[16,512]{1,0:T(8,128)S(1)} %get-tuple-element.3) | data formatting | bytes 65536

commit v5 on v4

--- a/solution.py
+++ b/solution.py
@@ -439,8 +439,8 @@
             remote(yf_send.at[slab(ys[k], 16)], yf_recv.at[y], yf_ss, yf_rs, yc[k], t).start()
 
     relay(0)
+    to_z(0)
     relay(1)
-    to_z(0)
     to_z(1)
     to_y()
     to_z(2)

time: 41.2 us -> 41.1 us (level)
  no operation moved by 1% of the time
where the time goes in v5:
time: 41.1 us; the launch traced here: 41 us
  Pallas kernels  39 us (95%)
  local copies, waits for them, and re-layouts  1.32 us (3%)
  between operations  0.64 us (2%)
    pallas_call x1, Pallas kernels, local(): pl.pallas_call(kernel, out_shape=outs, in_specs=[pl.BlockSpec(memory_spac...  39 us
    unnamed x2, local copies, waits for them, and re-layouts  1.32 us

profile of v5, /device:TPU:1, one launch (start us, length us, event | category | flops | bytes accessed | tf_op | source)
XLA Modules:
  0.0 41.0 jit_solution(5533922107957264622)
XLA Ops:
  0.6 39.0 %scan_backward.1 = (bf16[512,256]{1,0:T(8,128)(2,1)S(1)}, f32[16,512]{1,0:T(8,128)S(1)}) custom-call(bf16[512,256]{1,0:T(8,128)(2,1)} %lay_h.1, bf16[1024,512]{1,0:T(8,128)(2,1)} %vp_h.1, f32[4,512]{1,0:T(4,128)} %taps_h.1, bf16[512,512]{1,0:T(8,128)(2,1)} %pre_h.1, bf16[512,128]{1,0:T(8,128)(2,1)} %sin_h.1, bf16[512,128]{1,0:T(8,128)(2,1)} %sout_h.1, ...), custom_call_target="tpu_custom_call" | custom-call | flops 1500000000 | bytes 4000000 | tf_op jit(solution)/shard_map/scan_backward/pallas_call | solution.py:529
  39.6 0.7 %copy.14 = bf16[512,256]{1,0:T(8,128)(2,1)} copy(bf16[512,256]{1,0:T(8,128)(2,1)S(1)} %get-tuple-element.2) | data formatting | bytes 524288
  40.3 0.6 %copy.15 = f32[16,512]{1,0:T(8,128)} copy(f32[16,512]{1,0:T(8,128)S(1)} %get-tuple-element.3) | data formatting | bytes 65536
